TPU v7x, 32 devices: a whole 2x2x4 slice. The times are simulated.
32 devices in a mesh: row: 4 (over y, x), col: 8 (over z, core).
Axes of the slice: x: 2, y: 2, z: 4, core: 2. Of those that a mesh axis runs over, the one named last changes fastest.
Arguments:
- sign_iterate: bfloat16 [4096, 4096], P('row', 'col'), may hold values from -6 to 6
- sign_square: bfloat16 [4096, 4096], P('row', 'col'), may hold values from -0.1875 to 0.1875
- pattern_x: int32 [32, 32], P('row', 'col'), may hold values 0 or 1
- pattern_y: int32 [32, 32], P('row', 'col'), may hold values 0 or 1
- pattern_product: int32 [32, 32], P('row', 'col'), may hold values 0 or 1
- orbital_energy: bfloat16 [4096], P('row'), may hold values from -3 to 1
- pair_dest: int32 [32, 32, 1], P(('row', 'col')), may hold values from 0 to 31; in each aligned block of 32 rows (0 to 31, 32 to 63, ..., all dimensions but the last counted through in order) at most 2 rows name the same one
- pair_block: int32 [32, 32], P(('row', 'col')), may hold values from 0 to 31
- force_h: bfloat16 [2048, 128, 128], P(('row', 'col')), may hold values from -0.5 to 0.5
- force_s: bfloat16 [2048, 128, 128], P(('row', 'col')), may hold values from -0.5 to 0.5
Outputs:
- sign_next: bfloat16 [4096, 4096], P('row', 'col')
- forces: float32 [2048], P(('row', 'col'))
Inputs may be any that keep to these rules, and one draw needn't show every extreme that they name: `pair_dest`: among the 32 entries of one device no owner is named more than 2 times, a bound that some block reaches. `pair_block`: A row-major index into the device's own 8 x 4 grid of blocks.
All inputs are finite; a program needn't handle non-finite values. No bound on the sum of `pattern_x` or of `pattern_y` or of `pattern_product` on one device may be relied on, other than what follows from the above.
Results may differ from a plain program's by a relative error of at most 0.003.
Values may be sent and summed in bfloat16 or wider, within the bound.
A program may use at most 128 MiB of HBM per device.

v0:
```python
import jax
import jax.numpy as jnp
from jax import lax
from jax.sharding import PartitionSpec as P

BS = 128
QB = 4
CAP = 2


def masked_tile(tile, pattern):
    rows, cols = tile.shape
    shaped = tile.reshape(rows // BS, BS, cols // BS, BS) * pattern[:, None, :, None].astype(
        tile.dtype
    )
    return shaped.reshape(rows, cols)


def tile_blocks(tile):
    rows, cols = tile.shape
    shaped = tile.reshape(rows // BS, BS, cols // BS, BS).transpose(0, 2, 1, 3)
    return shaped.reshape(rows // BS * (cols // BS), BS * BS)


def rank_within(dest):
    entries = dest.shape[-1]
    order = jnp.arange(entries, dtype=jnp.int32)
    same = (dest[..., :, None] == dest[..., None, :]) & (order[None, :] < order[:, None])
    return jnp.sum(same.astype(jnp.int32), axis=-1)


def shards(
    sign_iterate,
    sign_square,
    pattern_x,
    pattern_y,
    pattern_product,
    orbital_energy,
    pair_dest,
    pair_block,
    force_h,
    force_s,
):
    rows_x, cols_x = sign_iterate.shape
    xmask = masked_tile(sign_iterate, pattern_x)
    ymask = masked_tile(sign_square, pattern_y)
    y_whole = lax.all_gather(ymask, "row", axis=0, tiled=True)
    product = jnp.dot(
        lax.all_gather(xmask, "col", axis=1, tiled=True),
        y_whole,
        preferred_element_type=jnp.float32,
    )
    product = masked_tile(product, pattern_product)
    xnew = 1.5 * xmask.astype(jnp.float32) - 0.5 * product
    sign_next = xnew.astype(jnp.bfloat16)
    global_rows = lax.axis_index("row") * rows_x + jnp.arange(rows_x, dtype=jnp.int32)
    global_cols = lax.axis_index("col") * cols_x + jnp.arange(cols_x, dtype=jnp.int32)
    identity = (global_rows[:, None] == global_cols[None, :]).astype(jnp.float32)
    density = (0.5 * identity - 0.5 * xnew).astype(jnp.bfloat16)
    dens_blocks = tile_blocks(density)
    n_rows = lax.axis_size("row")
    n_cols = lax.axis_size("col")
    devices = n_rows * n_cols
    slots = devices * CAP
    local_rows = rows_x // BS
    dest = pair_dest[0, :, 0]
    wanted = pair_block[0]
    rank = rank_within(dest)
    slot = dest * CAP + rank
    pick_slot = (jnp.arange(slots, dtype=jnp.int32)[:, None] == slot[None, :]).astype(jnp.bfloat16)
    pick_block = (
        wanted[:, None] == jnp.arange(dens_blocks.shape[0], dtype=jnp.int32)[None, :]
    ).astype(jnp.bfloat16)
    routing_table = jnp.dot(pick_slot, pick_block, preferred_element_type=jnp.float32).astype(
        jnp.bfloat16
    )
    send_dens = jnp.dot(routing_table, dens_blocks, preferred_element_type=jnp.float32).astype(
        jnp.bfloat16
    )
    pick_row = ((wanted // QB)[:, None] == jnp.arange(local_rows, dtype=jnp.int32)[None, :]).astype(
        jnp.bfloat16
    )
    slot_rows = jnp.dot(pick_slot, pick_row, preferred_element_type=jnp.float32).astype(
        jnp.bfloat16
    )
    send_energy = jnp.dot(
        slot_rows, orbital_energy.reshape(local_rows, BS), preferred_element_type=jnp.float32
    ).astype(jnp.bfloat16)
    payload = jnp.concatenate([send_dens.reshape(slots, BS, BS), send_energy[:, None, :]], axis=1)
    height = BS + 1
    received = lax.all_to_all(
        payload.reshape(devices, CAP, height * BS),
        ("row", "col"),
        split_axis=0,
        concat_axis=0,
        tiled=True,
    )
    received = received.reshape(slots, height, BS)
    recv_dens = received[:, :BS, :]
    energies = received[:, BS, :].astype(jnp.float32)
    h_term = jnp.einsum("sab,sab->s", recv_dens, force_h, preferred_element_type=jnp.float32)
    s_rows = jnp.einsum("sab,sab->sa", recv_dens, force_s, preferred_element_type=jnp.float32)
    forces = h_term - jnp.sum(energies * s_rows, axis=1)
    return (sign_next, forces)


def solution(mesh):
    in_specs = (
        P("row", "col"),
        P("row", "col"),
        P("row", "col"),
        P("row", "col"),
        P("row", "col"),
        P("row"),
        P(("row", "col"), None, None),
        P(("row", "col"), None),
        P(("row", "col"), None, None),
        P(("row", "col"), None, None),
    )
    out_specs = (P("row", "col"), P(("row", "col")))
    return jax.shard_map(shards, mesh=mesh, in_specs=in_specs, out_specs=out_specs, check_vma=False)
```

profile of v0, /device:TPU:1, one launch (start us, length us, event | category | flops | bytes accessed | tf_op | source)
XLA Modules:
  0.0 234.8 jit_solution(16649094409307848958)
XLA Ops:
  7.2 0.0 copy-start
  7.2 0.0 all-gather.5.cloned.1.call-start
  7.2 0.7 convert_element_type.48
  7.9 0.1 copy.22
  8.0 0.3 mul.72
  8.4 0.0 copy-start.4
  8.4 2.5 %bitcast_multiply_fusion.1 = bf16[1024,512]{1,0:T(8,128)(2,1)} fusion(bf16[1024,512]{1,0:T(8,128)(2,1)} %param.11, bf16[128,8,4,128]{3,2,1,0:T(4,128)(2,1)S(1)} %bitcast.38), kind=kLoop, calls=%fused_computation.17 | loop fusion | flops 524288 | bytes 3145728 | tf_op jit(solution)/shard_map/mul | solution.py:13
  10.9 0.0 all-gather.5.cloned.1.call-update
  10.9 0.0 all-gather.3.cloned.1.call-start
  11.0 0.1 copy.21
  11.1 0.3 mul.67
  11.4 0.0 copy-start.5
  11.4 1.1 bitcast_multiply_fusion.2
  12.6 0.0 all-gather.3.cloned.1.call-update
  12.6 0.1 copy.23
  12.7 0.2 convert_reduce_fusion
  12.9 0.4 fusion.5
  13.4 52.4 %all-gather.5.cloned.1.call-done = bf16[4096,512]{1,0:T(8,128)(2,1)} async-done(((bf16[1024,512]{1,0:T(8,128)(2,1)}), bf16[4096,512]{1,0:T(8,128)(2,1)}) %all-gather.5.cloned.1.call-update) | async-done | bytes 4194320 | tf_op jit(solution)/shard_map/all_gather | solution.py:47
  65.8 84.7 %all-gather.3.cloned.1.call-done = bf16[1024,4096]{1,0:T(8,128)(2,1)} async-done(((bf16[1024,512]{1,0:T(8,128)(2,1)}), bf16[1024,4096]{1,0:T(8,128)(2,1)}) %all-gather.3.cloned.1.call-update) | async-done | bytes 8388624 | tf_op jit(solution)/shard_map/all_gather | solution.py:49
  150.5 0.3 mul.75
  150.9 10.4 %subtract_convert_fusion = (bf16[1024,512]{1,0:T(8,128)(2,1)S(1)}, bf16[1024,512]{1,0:T(8,128)(2,1)}) fusion(s32[512]{0:T(512)S(1)} %iota_add_fusion.1, s32[1024]{0:T(1024)S(1)} %iota_add_fusion, f32[128,8,4,128]{3,2,1,0:T(4,128)S(1)} %bitcast.41, bf16[1024,4096]{1,0:T(8,128)(2,1)} %all-gather.3.cloned.1.call-done, ...), kind=kOutput, calls=%fused_computation.9 | convolution fusion | flops 4300734464 | bytes 17831936 | tf_op jit(solution)/shard_map/dot_general | solution.py:48
  161.3 0.3 reshape.86
  161.5 0.2 copy.24
  161.8 1.1 fusion.4
  162.9 0.6 copy.40
  163.5 0.2 pad_maximum_fusion
  163.7 2.2 reshape.90
  165.9 53.9 %all_to_all.5 = bf16[32,2,16512]{2,1,0:T(2,128)(2,1)} all-to-all(bf16[32,2,16512]{2,1,0:T(2,128)(2,1)} %reshape.90), channel_id=1, replica_groups=mesh['row'=4,'col'=8] {'row','col'}, dimensions={0} | all-to-all | bytes 4227072 | tf_op jit(solution)/shard_map/all_to_all | solution.py:91
  219.8 3.2 %reshape.91 = bf16[64,129,128]{2,1,0:T(8,128)(2,1)S(1)} reshape(bf16[32,2,16512]{2,1,0:T(2,128)(2,1)} %all_to_all.5) | data formatting | bytes 4227072 | tf_op jit(solution)/shard_map/reshape | solution.py:98
  223.0 4.2 %fusion.1 = (f32[64,128]{1,0:T(8,128)S(1)}, f32[64]{0:T(128)S(1)}) fusion(bf16[64,128,128]{2,1,0:T(8,128)(2,1)} %param.19, bf16[64,129,128]{2,1,0:T(8,128)(2,1)S(1)} %reshape.91, bf16[64,128,128]{2,1,0:T(8,128)(2,1)} %param.18), kind=kLoop, calls=%fused_computation.4 | loop fusion | flops 7331776 | bytes 6324480 | tf_op jit(solution)/shard_map/sab,sab->sa/dot_general | solution.py:102
  227.3 0.1 multiply_reduce_fusion
  227.4 0.5 sub.18
  (18 shorter events, 0.1 us)
Async XLA Ops:
  7.2 5.8 %copy-start = (bf16[1024]{0:T(1024)(128)(2,1)S(1)}, bf16[1024]{0:T(1024)(128)(2,1)}, u32[]{:S(2)}) copy-start(bf16[1024]{0:T(1024)(128)(2,1)} %param.15) | copy-start | bytes 6148
  7.2 58.6 %all-gather.5.cloned.1.call-start = ((), (), s32[]{:S(2)}) async-start(), calls=%async_computation.2 | async-start | bytes 5242880 | tf_op jit(solution)/shard_map/all_gather | solution.py:47
  8.4 2.6 %copy-start.4 = (s32[8,4]{0,1:T(4,128)S(1)}, s32[8,4]{0,1:T(4,128)}, u32[]{:S(2)}) copy-start(s32[8,4]{0,1:T(4,128)} %param.12) | copy-start | bytes 388
  8.4 3.1 %copy-start.2 = (bf16[1024,512]{1,0:T(8,128)(2,1)S(1)}, bf16[1024,512]{1,0:T(8,128)(2,1)}, u32[]{:S(2)}) copy-start(bf16[1024,512]{1,0:T(8,128)(2,1)} %param.10) | copy-start | bytes 3145732
  10.9 139.6 %all-gather.3.cloned.1.call-start = ((), (), s32[]{:S(2)}) async-start(), calls=%async_computation.1 | async-start | bytes 9437184 | tf_op jit(solution)/shard_map/all_gather | solution.py:49
  11.4 1.2 copy-start.5
  11.4 1.3 copy-start.6
  11.4 1.5 copy-start.3
  12.6 138.3 %copy-start.1 = (bf16[1024,512]{1,0:T(8,128)(2,1)S(1)}, bf16[1024,512]{1,0:T(8,128)(2,1)}, u32[]{:S(2)}) copy-start(bf16[1024,512]{1,0:T(8,128)(2,1)} %bitcast_multiply_fusion.2) | copy-start | bytes 3145732
Sparse Core Ops, SparseCore 0:
  11.0 54.7 all-gather.4
  68.0 82.4 all-gather.2
where the time goes:
time: 235 us
  waiting for transfers between devices  137 us (58%)
  blocking collectives  53.9 us (23%)
  between operations  14.3 us (6%)
  matrix products  11.9 us (5%)
  other arithmetic  9.61 us (4%)
  local copies, waits for them, and re-layouts  7.85 us (3%)
    all_gather x1, waiting for transfers between devices, shards(): lax.all_gather(xmask, 'col', axis=1, tiled=True)  84.7 us
    all_to_all x1, blocking collectives, shards(): lax.all_to_all(payload.reshape(devices, CAP, height * BS), ('row', 'col')...  53.9 us
    all_gather x1, waiting for transfers between devices, shards(): y_whole = lax.all_gather(ymask, 'row', axis=0, tiled=True)  52.4 us
    dot_general x1, matrix products, shards(): jnp.dot(lax.all_gather(xmask, 'col', axis=1, tiled=True), y_whole, prefer...  10.4 us
  transfers between devices with their start and end apart: 2, of which 2 were waited for; matrix products, arithmetic and copies ran while one was open for 1% of the time, Pallas kernels for 0%

commit v1 on v0

--- a/solution.py
+++ b/solution.py
@@ -1,11 +1,14 @@
 import jax
 import jax.numpy as jnp
 from jax import lax
+from jax.experimental import pallas as pl
+from jax.experimental.pallas import tpu as pltpu
 from jax.sharding import PartitionSpec as P
 
 BS = 128
 QB = 4
 CAP = 2
+MESH = pl.DeviceIdType.MESH
 
 
 def masked_tile(tile, pattern):
@@ -104,6 +107,436 @@
     return (sign_next, forces)
 
 
+ROWS = 4
+COLS = 8
+DEVICES = ROWS * COLS
+LINE = 4
+CHUNKS = 4
+STEP = 256
+HALF = 512
+
+
+def kernel(
+    pat,
+    table,
+    energy,
+    x_hbm,
+    y_hbm,
+    h_hbm,
+    s_hbm,
+    sign_hbm,
+    parts,
+    xg,
+    yg,
+    acc,
+    dens,
+    sgn,
+    hbuf,
+    sbuf,
+    wbuf,
+    outbox,
+    inbox,
+    e_out,
+    e_in,
+    local_sem,
+    up_sem,
+    down_sem,
+    twin_sem,
+    x_sem,
+    ysend_sem,
+    y_sem,
+    e_sem,
+    esend_sem,
+    d_sem,
+    dsend_sem,
+):
+    r = lax.axis_index("row")
+    c = lax.axis_index("col")
+    me = r * COLS + c
+    z = c // 2
+    core = c % 2
+    row_x = r + 1 - 2 * (r % 2)
+    row_y = (r + 2) % 4
+
+    barrier = pltpu.get_barrier_semaphore()
+
+    def greet(i, carry):
+        other = (me + i) % DEVICES
+        pl.semaphore_signal(
+            barrier, inc=1, device_id=(other // COLS, other % COLS), device_id_type=MESH
+        )
+        return carry
+
+    lax.fori_loop(1, DEVICES, greet, 0)
+
+    get_x = pltpu.make_async_copy(x_hbm, xg.at[c], local_sem.at[0])
+    get_y = pltpu.make_async_copy(y_hbm, yg.at[r], local_sem.at[1])
+    get_h = pltpu.make_async_copy(h_hbm, hbuf, local_sem.at[2])
+    get_s = pltpu.make_async_copy(s_hbm, sbuf, local_sem.at[3])
+    get_x.start()
+    get_y.start()
+    get_h.start()
+    get_s.start()
+
+    def mask(ref, slot, base, ch):
+        for i in range(STEP // BS):
+            rows = pl.ds(ch * STEP + i * BS, BS)
+            for j in range(QB):
+                keep = pat[base + j, ch * (STEP // BS) + i].astype(jnp.float32)
+                block = ref[slot, rows, j * BS : (j + 1) * BS].astype(jnp.float32)
+                ref[slot, rows, j * BS : (j + 1) * BS] = (block * keep).astype(jnp.bfloat16)
+
+    def x_copy(panel, ch, where, send_sem):
+        block = xg.at[panel, pl.ds(ch * STEP, STEP)]
+        return pltpu.make_async_remote_copy(
+            src_ref=block,
+            dst_ref=block,
+            send_sem=send_sem.at[panel // 2, ch],
+            recv_sem=x_sem.at[panel, ch],
+            device_id=(r, where),
+            device_id_type=MESH,
+        )
+
+    def up(panel, ch):
+        return x_copy(panel, ch, c + 2, up_sem)
+
+    def down(panel, ch):
+        return x_copy(panel, ch, c - 2, down_sem)
+
+    def twin(panel, ch):
+        return x_copy(panel, ch, c + 1 - 2 * core, twin_sem)
+
+    def y_copy(owner, half, to, number):
+        block = yg.at[owner, pl.ds(half * HALF, HALF)]
+        return pltpu.make_async_remote_copy(
+            src_ref=block,
+            dst_ref=block,
+            send_sem=ysend_sem.at[number],
+            recv_sem=y_sem.at[owner, half],
+            device_id=(to, c),
+            device_id_type=MESH,
+        )
+
+    get_x.wait()
+    mask(xg, c, 0, 0)
+    pl.semaphore_wait(barrier, DEVICES - 1)
+
+    def send_x(ch):
+        @pl.when(z < LINE - 1)
+        def _():
+            up(c, ch).start()
+
+        @pl.when(z > 0)
+        def _():
+            down(c, ch).start()
+
+        twin(c, ch).start()
+
+    send_x(0)
+    get_y.wait()
+
+    def mask_y(ch, carry):
+        mask(yg, r, QB, ch)
+        return carry
+
+    lax.fori_loop(0, CHUNKS, mask_y, 0)
+    y_copy(r, 0, row_x, 0).start()
+    y_copy(r, 1, row_y, 1).start()
+    y_copy(r, 1, row_x, 2).start()
+    y_copy(r, 0, row_y, 3).start()
+
+    def start_x(ch, carry):
+        mask(xg, c, 0, ch)
+        send_x(ch)
+        return carry
+
+    lax.fori_loop(1, CHUNKS, start_x, 0)
+
+    def pack_energy(o, carry):
+        for k in range(CAP):
+            e_out[o, k : k + 1, :] = energy[pl.ds(table[0, o * CAP + k] // QB, 1), :]
+        for k in range(CAP, 8):
+            e_out[o, k : k + 1, :] = jnp.zeros((1, BS), jnp.float32)
+        return carry
+
+    lax.fori_loop(0, DEVICES, pack_energy, 0)
+
+    def e_copy(o):
+        return pltpu.make_async_remote_copy(
+            src_ref=e_out.at[o],
+            dst_ref=e_in.at[me],
+            send_sem=esend_sem,
+            recv_sem=e_sem,
+            device_id=(o // COLS, o % COLS),
+            device_id_type=MESH,
+        )
+
+    def send_energy(i, carry):
+        e_copy((me + i) % DEVICES).start()
+        return carry
+
+    lax.fori_loop(1, DEVICES, send_energy, 0)
+    pltpu.make_async_copy(e_out.at[me], e_in.at[me], e_sem).start()
+
+    dens[QB * 8] = jnp.zeros((BS, BS), jnp.bfloat16)
+    get_h.wait()
+    get_s.wait()
+    pltpu.make_async_copy(e_in, e_in, e_sem).wait()
+
+    eye = lax.broadcasted_iota(jnp.int32, (BS, BS), 0) == lax.broadcasted_iota(
+        jnp.int32, (BS, BS), 1
+    )
+
+    def weigh(src, carry):
+        for k in range(CAP):
+            line = jnp.broadcast_to(e_in[src, k : k + 1, :], (BS, BS))
+            col = jnp.sum(jnp.where(eye, line, 0.0), axis=1, keepdims=True)
+            s = src * CAP + k
+            wbuf[s] = hbuf[s].astype(jnp.float32) - col * sbuf[s].astype(jnp.float32)
+        return carry
+
+    lax.fori_loop(0, DEVICES, weigh, 0)
+
+    def pass_on(d, ch):
+        @pl.when(z >= d)
+        def _():
+            panel = c - 2 * d
+            x_copy(panel, ch, c, up_sem).wait_recv()
+
+            @pl.when(z < LINE - 1)
+            def _():
+                up(panel, ch).start()
+
+            twin(panel, ch).start()
+
+        @pl.when(z + d < LINE)
+        def _():
+            panel = c + 2 * d
+            x_copy(panel, ch, c, down_sem).wait_recv()
+
+            @pl.when(z > 0)
+            def _():
+                down(panel, ch).start()
+
+            twin(panel, ch).start()
+
+    def wait_twin(zp, ch):
+        x_copy(2 * zp + 1 - core, ch, c, twin_sem).wait_recv()
+
+    def multiply(zp, ch):
+        rows = pl.ds(ch * STEP, STEP)
+        return jnp.dot(
+            xg[2 * zp, rows, :], yg[zp, 0:HALF, :], preferred_element_type=jnp.float32
+        ) + jnp.dot(
+            xg[2 * zp + 1, rows, :], yg[zp, HALF : 2 * HALF, :], preferred_element_type=jnp.float32
+        )
+
+    def add(d, ch):
+        rows = pl.ds(ch * STEP, STEP)
+
+        @pl.when(z >= d)
+        def _():
+            wait_twin(z - d, ch)
+            acc[rows, :] += multiply(z - d, ch)
+
+        @pl.when(z + d < LINE)
+        def _():
+            wait_twin(z + d, ch)
+            acc[rows, :] += multiply(z + d, ch)
+
+    def loop(lo, hi, body):
+        def step(i, carry):
+            body(i)
+            return carry
+
+        lax.fori_loop(lo, hi, step, 0)
+
+    loop(0, 2, lambda ch: pass_on(1, ch))
+    y_copy(row_x, 0, r, 0).wait_recv()
+    y_copy(row_x, 0, row_y, 4).start()
+    y_copy(row_y, 1, r, 1).wait_recv()
+    y_copy(row_y, 1, row_x, 5).start()
+    loop(2, CHUNKS, lambda ch: pass_on(1, ch))
+    loop(0, 2, lambda ch: pass_on(2, ch))
+    y_copy(row_x, 1, r, 2).wait_recv()
+    y_copy(row_y, 0, r, 3).wait_recv()
+    row_d = 3 - r
+    y_copy(row_d, 0, r, 4).wait_recv()
+    y_copy(row_d, 1, r, 5).wait_recv()
+
+    def first(ch):
+        wait_twin(z, ch)
+        acc[pl.ds(ch * STEP, STEP), :] = multiply(z, ch)
+
+    loop(0, CHUNKS, first)
+    loop(0, CHUNKS, lambda ch: add(1, ch))
+    loop(2, CHUNKS, lambda ch: pass_on(2, ch))
+    loop(0, CHUNKS, lambda ch: add(2, ch))
+
+    eye_f = eye.astype(jnp.float32)
+
+    def finish(ch):
+        for i in range(STEP // BS):
+            block_row = ch * (STEP // BS) + i
+            rows = pl.ds(ch * STEP + i * BS, BS)
+            for j in range(QB):
+                cols = slice(j * BS, (j + 1) * BS)
+                keep = pat[2 * QB + j, block_row].astype(jnp.float32)
+                xnew = 1.5 * xg[c, rows, cols].astype(jnp.float32) - 0.5 * (acc[rows, cols] * keep)
+                sgn[rows, cols] = xnew.astype(jnp.bfloat16)
+                on = jnp.where(r * 8 + block_row == c * QB + j, 0.5, 0.0).astype(jnp.float32)
+                dens[block_row * QB + j] = (on * eye_f - 0.5 * xnew).astype(jnp.bfloat16)
+
+    pass_on(3, 0)
+
+    def last(ch):
+        pass_on(3, ch)
+        add(3, ch - 1)
+        finish(ch - 1)
+
+    loop(1, CHUNKS, last)
+    add(3, CHUNKS - 1)
+    finish(CHUNKS - 1)
+
+    put = pltpu.make_async_copy(sgn, sign_hbm, local_sem.at[4])
+    put.start()
+
+    def d_copy(o, src):
+        return pltpu.make_async_remote_copy(
+            src_ref=outbox.at[o],
+            dst_ref=inbox.at[src],
+            send_sem=dsend_sem,
+            recv_sem=d_sem.at[src],
+            device_id=(o // COLS, o % COLS),
+            device_id_type=MESH,
+        )
+
+    flips = (3 - z, (z + 2) % LINE, z + 1 - 2 * (z % 2), z)
+    for n, zz in enumerate(flips):
+
+        def send(j, zz=zz):
+            o = (r + j // 2) % ROWS * COLS + zz * 2 + (core + j) % 2
+            for k in range(CAP):
+                outbox[o, k] = dens[table[0, o * CAP + k]]
+            d_copy(o, me).start()
+
+        loop(0 if n < 3 else 1, COLS, send)
+
+    def force(s, block):
+        parts[pl.ds(s, 1), :] = jnp.sum(block.astype(jnp.float32) * wbuf[s], axis=0, keepdims=True)
+
+    for k in range(CAP):
+        force(me * CAP + k, dens[table[0, me * CAP + k]])
+
+    for n in (3, 2, 1, 0):
+
+        def take(j, zz=flips[n]):
+            src = (r + ROWS - j // 2) % ROWS * COLS + zz * 2 + (core + j) % 2
+            d_copy(src, src).wait_recv()
+            for k in range(CAP):
+                force(src * CAP + k, inbox[src, k])
+
+        loop(0 if n < 3 else 1, COLS, take)
+
+    def sent(ch):
+        for zp in range(LINE):
+            panel = 2 * zp + core
+
+            @pl.when((z >= zp) & (z < LINE - 1))
+            def _():
+                up(panel, ch).wait_send()
+
+            @pl.when((z <= zp) & (z > 0))
+            def _():
+                down(panel, ch).wait_send()
+
+            twin(panel, ch).wait_send()
+
+    loop(0, CHUNKS, sent)
+    y_copy(r, 0, row_x, 0).wait_send()
+    y_copy(r, 1, row_y, 1).wait_send()
+    y_copy(r, 1, row_x, 2).wait_send()
+    y_copy(r, 0, row_y, 3).wait_send()
+    y_copy(row_x, 0, row_y, 4).wait_send()
+    y_copy(row_y, 1, row_x, 5).wait_send()
+    out = e_out.at[pl.ds(0, DEVICES - 1)]
+    pltpu.make_async_copy(out, out, esend_sem).wait()
+    out = outbox.at[pl.ds(0, DEVICES - 1)]
+    pltpu.make_async_copy(out, out, dsend_sem).wait()
+    put.wait()
+
+
+def fused(
+    sign_iterate,
+    sign_square,
+    pattern_x,
+    pattern_y,
+    pattern_product,
+    orbital_energy,
+    pair_dest,
+    pair_block,
+    force_h,
+    force_s,
+):
+    slots = DEVICES * CAP
+    dest = pair_dest[0, :, 0]
+    slot = dest * CAP + rank_within(dest)
+    none = sign_iterate.shape[0] // BS * QB
+    named = slot[:, None] == jnp.arange(slots, dtype=jnp.int32)[None, :]
+    table = none - jnp.sum(
+        jnp.where(named, none - pair_block[0][:, None], 0), axis=0, keepdims=True
+    )
+    pat = jnp.concatenate([pattern_x.T, pattern_y.T, pattern_product.T], axis=0)
+    energy = orbital_energy.reshape(-1, BS).astype(jnp.float32)
+    energy = jnp.concatenate([energy, jnp.zeros_like(energy)], axis=0)
+    vmem = pl.BlockSpec(memory_space=pltpu.VMEM)
+    smem = pl.BlockSpec(memory_space=pltpu.SMEM)
+    hbm = pl.BlockSpec(memory_space=pl.ANY)
+    bf16, f32 = jnp.bfloat16, jnp.float32
+    dma = pltpu.SemaphoreType.DMA
+    sign_next, parts = pl.pallas_call(
+        kernel,
+        out_shape=(
+            jax.ShapeDtypeStruct(sign_iterate.shape, bf16),
+            jax.ShapeDtypeStruct((slots, BS), f32),
+        ),
+        in_specs=[smem, smem, vmem, hbm, hbm, hbm, hbm],
+        out_specs=(hbm, vmem),
+        scratch_shapes=[
+            pltpu.VMEM((COLS, 1024, 512), bf16),
+            pltpu.VMEM((ROWS, 1024, 512), bf16),
+            pltpu.VMEM((1024, 512), f32),
+            pltpu.VMEM((none + 1, BS, BS), bf16),
+            pltpu.VMEM((1024, 512), bf16),
+            pltpu.VMEM((slots, BS, BS), bf16),
+            pltpu.VMEM((slots, BS, BS), bf16),
+            pltpu.VMEM((slots, BS, BS), f32),
+            pltpu.VMEM((DEVICES, CAP, BS, BS), bf16),
+            pltpu.VMEM((DEVICES, CAP, BS, BS), bf16),
+            pltpu.VMEM((DEVICES, 8, BS), f32),
+            pltpu.VMEM((DEVICES, 8, BS), f32),
+            dma((5,)),
+            dma((LINE, CHUNKS)),
+            dma((LINE, CHUNKS)),
+            dma((LINE, CHUNKS)),
+            dma((COLS, CHUNKS)),
+            dma((6,)),
+            dma((ROWS, 2)),
+            dma,
+            dma,
+            dma((DEVICES,)),
+            dma,
+        ],
+        compiler_params=pltpu.CompilerParams(
+            collective_id=0, has_side_effects=True, vmem_limit_bytes=48 * 1024 * 1024
+        ),
+        cost_estimate=pl.CostEstimate(
+            flops=2 * 1024 * 4096 * 512, bytes_accessed=8 * 1024 * 1024, transcendentals=0
+        ),
+    )(pat, table, energy, sign_iterate, sign_square, force_h, force_s)
+    return sign_next, jnp.sum(parts, axis=1)
+
+
 def solution(mesh):
     in_specs = (
         P("row", "col"),
@@ -118,4 +551,5 @@
         P(("row", "col"), None, None),
     )
     out_specs = (P("row", "col"), P(("row", "col")))
-    return jax.shard_map(shards, mesh=mesh, in_specs=in_specs, out_specs=out_specs, check_vma=False)
+    body = fused if (mesh.shape["row"], mesh.shape["col"]) == (ROWS, COLS) else shards
+    return jax.shard_map(body, mesh=mesh, in_specs=in_specs, out_specs=out_specs, check_vma=False)

time: 235 us -> 147 us (0.63)
  waiting for transfers between devices: 137 us -> 0 us
  Pallas kernels: 0 us -> 136 us
  blocking collectives: 53.9 us -> 0 us
  between operations: 14.3 us -> 0.64 us
  matrix products: 11.9 us -> 0 us
  other arithmetic: 9.61 us -> 4.36 us
  local copies, waits for them, and re-layouts: 7.85 us -> 5.01 us
    all_gather x2 -> x0, waiting for transfers between devices: 137 us -> none  [the longest x1 84.7 us: shards(): lax.all_gather(xmask, 'col', axis=1, tiled=True)]
    pallas_call x0 -> x1, Pallas kernels: none -> 136 us  [fused(): pl.pallas_call(kernel, out_shape=(jax.ShapeDtypeStruct(sign_iterate.shape...]
    all_to_all x1 -> x0, blocking collectives: 53.9 us -> none  [shards(): lax.all_to_all(payload.reshape(devices, CAP, height * BS), ('row', 'col')...]
    dot_general x3 -> x0, matrix products: 11.9 us -> none  [the longest x1 10.4 us: shards(): jnp.dot(lax.all_gather(xmask, 'col', axis=1, tiled=True), y_whole, prefer...]
    reshape x4 -> x0, local copies, waits for them, and re-layouts: 5.91 us -> none  [the longest x1 3.17 us: shards(): received = received.reshape(slots, height, BS)]
    unnamed x15 -> x7, local copies, waits for them, and re-layouts: 0.61 us -> 5.01 us
    dot_general x1 -> x0, other arithmetic: 4.24 us -> none  [shards(): jnp.einsum('sab,sab->sa', recv_dens, force_s, preferred_element_type=jnp....]
    mul x2 -> x0, other arithmetic: 3.62 us -> none  [masked_tile(): tile.reshape(rows // BS, BS, cols // BS, BS)]
  transfers between devices with their start and end apart: 2 -> 0, of which waited for: 2 -> 0; matrix products, arithmetic and copies ran while one was open for 1% -> 0% of each run, Pallas kernels for 0% -> 0%
where the time goes in v1:
time: 147 us; the launch traced here: 146 us
  Pallas kernels  136 us (93%)
  local copies, waits for them, and re-layouts  5.01 us (3%)
  other arithmetic  4.36 us (3%)
    pallas_call x1, Pallas kernels, fused(): pl.pallas_call(kernel, out_shape=(jax.ShapeDtypeStruct(sign_iterate.shape...  136 us
    unnamed x7, local copies, waits for them, and re-layouts  5.01 us

profile of v1, /device:TPU:1, one launch (start us, length us, event | category | flops | bytes accessed | tf_op | source)
XLA Modules:
  0.0 145.8 jit_solution(16276942110374725934)
XLA Ops:
  0.6 0.7 subtract_bitcast_fusion.1
  1.3 0.9 convert_reduce_fusion
  2.2 0.7 multiply_add_fusion
  2.9 0.1 select_reduce_fusion
  3.0 0.7 pad_add_fusion.pat
  3.7 0.7 pad_convert_fusion.energy
  4.4 0.0 copy-start
  4.4 1.6 %copy-done = bf16[64,128,128]{2,1,0:T(8,128)(2,1)S(1)} copy-done((bf16[64,128,128]{2,1,0:T(8,128)(2,1)S(1)}, bf16[64,128,128]{2,1,0:T(8,128)(2,1)}, u32[]{:S(2)}) %copy-start) | copy-done | bytes 2097176
  6.0 0.0 copy-start.1
  6.0 1.2 copy-done.1
  7.2 0.0 copy-start.2
  7.2 1.2 copy-done.2
  8.4 135.7 %shard_map.113 = (bf16[1024,512]{1,0:T(8,128)(2,1)S(1)}, f32[64,128]{1,0:T(8,128)S(1)}) custom-call(s32[12,8]{1,0:T(8,128)S(1)} %pad_add_fusion.pat, s32[1,64]{1,0:T(1,128)S(1)} %subtract_bitcast_fusion.table, f32[16,128]{1,0:T(8,128)S(1)} %pad_convert_fusion.energy, bf16[1024,512]{1,0:T(8,128)(2,1)S(1)} %copy-done.1, bf16[1024,512]{1,0:T(8,128)(2,1)S(1)} %copy-done.2, ...), custom_call_target="tpu_custom_call" | custom-call | flops 4294967296 | bytes 8388608 | tf_op jit(solution)/shard_map/pallas_call | solution.py:497
  144.2 0.6 reduce_sum.29
  144.8 1.0 copy.13
  (1 shorter events, 0.0 us)
Async XLA Ops:
  4.4 1.6 %copy-start = (bf16[64,128,128]{2,1,0:T(8,128)(2,1)S(1)}, bf16[64,128,128]{2,1,0:T(8,128)(2,1)}, u32[]{:S(2)}) copy-start(bf16[64,128,128]{2,1,0:T(8,128)(2,1)} %h_hbm.1) | copy-start | bytes 6291460
  6.0 1.2 copy-start.1
  7.2 1.2 copy-start.2

commit v2 on v1

--- a/solution.py
+++ b/solution.py
@@ -1,3 +1,5 @@
+import functools
+
 import jax
 import jax.numpy as jnp
 from jax import lax
@@ -112,13 +114,19 @@
 DEVICES = ROWS * COLS
 LINE = 4
 CHUNKS = 4
+TALL = 8
 STEP = 256
 HALF = 512
 
 
 def kernel(
-    pat,
-    table,
+    room,
+    pat_x,
+    pat_y,
+    pat_p,
+    dest,
+    wanted,
+    pat_tile,
     energy,
     x_hbm,
     y_hbm,
@@ -126,6 +134,9 @@
     s_hbm,
     sign_hbm,
     parts,
+    xraw,
+    lines,
+    twins,
     xg,
     yg,
     acc,
@@ -138,18 +149,30 @@
     inbox,
     e_out,
     e_in,
+    e_rows,
+    t_out,
+    t_in,
+    pats,
+    ahead,
+    listed,
+    place,
+    table,
     local_sem,
     up_sem,
     down_sem,
     twin_sem,
     x_sem,
+    tx_sem,
     ysend_sem,
     y_sem,
     e_sem,
     esend_sem,
     d_sem,
     dsend_sem,
+    t_sem,
+    tsend_sem,
 ):
+    chunk = room // CHUNKS
     r = lax.axis_index("row")
     c = lax.axis_index("col")
     me = r * COLS + c
@@ -169,42 +192,49 @@
 
     lax.fori_loop(1, DEVICES, greet, 0)
 
-    get_x = pltpu.make_async_copy(x_hbm, xg.at[c], local_sem.at[0])
+    for j in range(QB):
+        pltpu.make_async_copy(
+            x_hbm.at[:, :, j * BS : (j + 1) * BS],
+            xraw.at[pl.ds(j * TALL, TALL)],
+            local_sem.at[0],
+        ).start()
+    get_x = pltpu.make_async_copy(xraw, xraw, local_sem.at[0])
     get_y = pltpu.make_async_copy(y_hbm, yg.at[r], local_sem.at[1])
     get_h = pltpu.make_async_copy(h_hbm, hbuf, local_sem.at[2])
     get_s = pltpu.make_async_copy(s_hbm, sbuf, local_sem.at[3])
-    get_x.start()
     get_y.start()
     get_h.start()
     get_s.start()
 
-    def mask(ref, slot, base, ch):
-        for i in range(STEP // BS):
-            rows = pl.ds(ch * STEP + i * BS, BS)
-            for j in range(QB):
-                keep = pat[base + j, ch * (STEP // BS) + i].astype(jnp.float32)
-                block = ref[slot, rows, j * BS : (j + 1) * BS].astype(jnp.float32)
-                ref[slot, rows, j * BS : (j + 1) * BS] = (block * keep).astype(jnp.bfloat16)
-
-    def x_copy(panel, ch, where, send_sem):
-        block = xg.at[panel, pl.ds(ch * STEP, STEP)]
+    def loop(lo, hi, body):
+        def step(i, carry):
+            body(i)
+            return carry
+
+        lax.fori_loop(lo, hi, step, 0)
+
+    def x_copy(src, dst, ch, col, send_sem, recv_sem):
+        rows = pl.ds(ch * chunk, chunk)
         return pltpu.make_async_remote_copy(
-            src_ref=block,
-            dst_ref=block,
-            send_sem=send_sem.at[panel // 2, ch],
-            recv_sem=x_sem.at[panel, ch],
-            device_id=(r, where),
+            src_ref=src.at[rows],
+            dst_ref=dst.at[rows],
+            send_sem=send_sem,
+            recv_sem=recv_sem,
+            device_id=(r, col),
             device_id_type=MESH,
         )
 
-    def up(panel, ch):
-        return x_copy(panel, ch, c + 2, up_sem)
-
-    def down(panel, ch):
-        return x_copy(panel, ch, c - 2, down_sem)
-
-    def twin(panel, ch):
-        return x_copy(panel, ch, c + 1 - 2 * core, twin_sem)
+    def up(d, ch):
+        return x_copy(lines[d], lines[d + 1], ch, c + 2, up_sem.at[d, ch], x_sem.at[d + 1, ch])
+
+    def down(d, ch):
+        src = lines[d + LINE - 1] if d else lines[0]
+        to = d + LINE
+        return x_copy(src, lines[to], ch, c - 2, down_sem.at[d, ch], x_sem.at[to, ch])
+
+    def twin(i, ch):
+        other = c + 1 - 2 * core
+        return x_copy(lines[i], twins[i], ch, other, twin_sem.at[i, ch], tx_sem.at[i, ch])
 
     def y_copy(owner, half, to, number):
         block = yg.at[owner, pl.ds(half * HALF, HALF)]
@@ -217,46 +247,104 @@
             device_id_type=MESH,
         )
 
+    t_out[...] = jnp.zeros_like(t_out)
+    t_out[0:QB, 0:TALL] = pat_tile[...]
+    blocks = QB * TALL
+    number = jnp.int32(0)
+    spots = []
+    for b in range(blocks):
+        on = pat_x[b // TALL, b % TALL]
+        spots.append(on * number + (1 - on) * blocks)
+        number = number + on
+    count = number
+    for b in range(blocks):
+        ahead[b] = spots[b]
+
+    def seek(t):
+        found = jnp.int32(0)
+        for b in range(blocks):
+            found = found + (ahead[b] == t).astype(jnp.int32) * b
+        listed[t] = found
+
+    loop(0, room, seek)
     get_x.wait()
-    mask(xg, c, 0, 0)
+
+    def compact(t):
+        lines[0][t] = xraw[listed[t]]
+
+    loop(0, room, compact)
     pl.semaphore_wait(barrier, DEVICES - 1)
+
+    def t_copy(col):
+        return pltpu.make_async_remote_copy(
+            src_ref=t_out,
+            dst_ref=t_in.at[c],
+            send_sem=tsend_sem,
+            recv_sem=t_sem,
+            device_id=(r, col),
+            device_id_type=MESH,
+        )
+
+    loop(1, COLS, lambda i: t_copy((c + i) % COLS).start())
+    pltpu.make_async_copy(t_out, t_in.at[c], t_sem).start()
 
     def send_x(ch):
         @pl.when(z < LINE - 1)
         def _():
-            up(c, ch).start()
+            up(0, ch).start()
 
         @pl.when(z > 0)
         def _():
-            down(c, ch).start()
-
-        twin(c, ch).start()
-
-    send_x(0)
+            down(0, ch).start()
+
+        twin(0, ch).start()
+
+    loop(0, CHUNKS, send_x)
     get_y.wait()
 
-    def mask_y(ch, carry):
-        mask(yg, r, QB, ch)
-        return carry
-
-    lax.fori_loop(0, CHUNKS, mask_y, 0)
+    def mask_y(i):
+        rows = pl.ds(i * BS, BS)
+        for j in range(QB):
+            cols = slice(j * BS, (j + 1) * BS)
+            keep = pat_y[j, i].astype(jnp.float32)
+            yg[r, rows, cols] = (yg[r, rows, cols].astype(jnp.float32) * keep).astype(jnp.bfloat16)
+
+    loop(0, TALL, mask_y)
     y_copy(r, 0, row_x, 0).start()
     y_copy(r, 1, row_y, 1).start()
     y_copy(r, 1, row_x, 2).start()
     y_copy(r, 0, row_y, 3).start()
 
-    def start_x(ch, carry):
-        mask(xg, c, 0, ch)
-        send_x(ch)
-        return carry
-
-    lax.fori_loop(1, CHUNKS, start_x, 0)
+    def mask_x(i):
+        rows = pl.ds(i * BS, BS)
+        for j in range(QB):
+            keep = pat_x[j, i].astype(jnp.float32)
+            block = xraw[j * TALL + i].astype(jnp.float32) * keep
+            xg[c, rows, j * BS : (j + 1) * BS] = block.astype(jnp.bfloat16)
+
+    loop(0, TALL, mask_x)
+
+    def find(o):
+        seen = jnp.int32(0)
+        slots = [jnp.int32(blocks)] * CAP
+        for p in range(dest.shape[1]):
+            hit = (dest[0, p] == o).astype(jnp.int32)
+            for k in range(CAP):
+                first_seen = hit * (seen == k).astype(jnp.int32)
+                slots[k] = slots[k] + first_seen * (wanted[0, p] - blocks)
+            seen = seen + hit
+        for k in range(CAP):
+            table[o * CAP + k] = slots[k]
+
+    loop(0, DEVICES, find)
+    e_rows[0:TALL, :] = energy[...].astype(jnp.float32)
+    e_rows[TALL : 2 * TALL, :] = jnp.zeros((TALL, BS), jnp.float32)
 
     def pack_energy(o, carry):
         for k in range(CAP):
-            e_out[o, k : k + 1, :] = energy[pl.ds(table[0, o * CAP + k] // QB, 1), :]
+            e_out[o, k : k + 1, :] = e_rows[pl.ds(table[o * CAP + k] // QB, 1), :]
         for k in range(CAP, 8):
-            e_out[o, k : k + 1, :] = jnp.zeros((1, BS), jnp.float32)
+            e_out[o, k : k + 1, :] = jnp.full((1, BS), count.astype(jnp.float32))
         return carry
 
     lax.fori_loop(0, DEVICES, pack_energy, 0)
@@ -297,31 +385,60 @@
 
     lax.fori_loop(0, DEVICES, weigh, 0)
 
+    most = e_in[0]
+    for src in range(1, DEVICES):
+        most = jnp.maximum(most, e_in[src])
+    parts[DEVICES * CAP : DEVICES * CAP + 8, :] = jnp.broadcast_to(most[CAP : CAP + 1, :], (8, BS))
+
+    pltpu.make_async_copy(t_in, t_in, t_sem).wait()
+    get_pats = pltpu.make_async_copy(t_in, pats, local_sem.at[5])
+    get_pats.start()
+    get_pats.wait()
+
+    for ref in (*lines, *twins):
+        ref[blocks] = jnp.zeros((BS, BS), jnp.bfloat16)
+
+    def locate(panel):
+        number = jnp.int32(0)
+        for b in range(blocks):
+            on = pats[panel, b // TALL, b % TALL]
+            place[panel, b] = on * number + (1 - on) * blocks
+            number = number + on
+
+    loop(0, COLS, locate)
+
     def pass_on(d, ch):
         @pl.when(z >= d)
         def _():
-            panel = c - 2 * d
-            x_copy(panel, ch, c, up_sem).wait_recv()
-
-            @pl.when(z < LINE - 1)
-            def _():
-                up(panel, ch).start()
-
-            twin(panel, ch).start()
+            up(d - 1, ch).wait_recv()
+            if d < LINE - 1:
+
+                @pl.when(z < LINE - 1)
+                def _():
+                    up(d, ch).start()
+
+            twin(d, ch).start()
 
         @pl.when(z + d < LINE)
         def _():
-            panel = c + 2 * d
-            x_copy(panel, ch, c, down_sem).wait_recv()
-
-            @pl.when(z > 0)
-            def _():
-                down(panel, ch).start()
-
-            twin(panel, ch).start()
-
-    def wait_twin(zp, ch):
-        x_copy(2 * zp + 1 - core, ch, c, twin_sem).wait_recv()
+            down(d - 1, ch).wait_recv()
+            if d < LINE - 1:
+
+                @pl.when(z > 0)
+                def _():
+                    down(d, ch).start()
+
+            twin(LINE - 1 + d, ch).start()
+
+    def wait_twin(i):
+        loop(0, CHUNKS, lambda ch: twin(i, ch).wait_recv())
+
+    def expand(ref, panel, ch):
+        for i in range(STEP // BS):
+            row = ch * (STEP // BS) + i
+            for j in range(QB):
+                block = ref[place[panel, j * TALL + row]]
+                xg[panel, pl.ds(row * BS, BS), j * BS : (j + 1) * BS] = block
 
     def multiply(zp, ch):
         rows = pl.ds(ch * STEP, STEP)
@@ -331,25 +448,24 @@
             xg[2 * zp + 1, rows, :], yg[zp, HALF : 2 * HALF, :], preferred_element_type=jnp.float32
         )
 
-    def add(d, ch):
-        rows = pl.ds(ch * STEP, STEP)
+    def add(d):
+        def panels(zp, i):
+            wait_twin(i)
+
+            def one(ch):
+                expand(lines[i], 2 * zp + core, ch)
+                expand(twins[i], 2 * zp + 1 - core, ch)
+                acc[pl.ds(ch * STEP, STEP), :] += multiply(zp, ch)
+
+            loop(0, CHUNKS, one)
 
         @pl.when(z >= d)
         def _():
-            wait_twin(z - d, ch)
-            acc[rows, :] += multiply(z - d, ch)
+            panels(z - d, d)
 
         @pl.when(z + d < LINE)
         def _():
-            wait_twin(z + d, ch)
-            acc[rows, :] += multiply(z + d, ch)
-
-    def loop(lo, hi, body):
-        def step(i, carry):
-            body(i)
-            return carry
-
-        lax.fori_loop(lo, hi, step, 0)
+            panels(z + d, LINE - 1 + d)
 
     loop(0, 2, lambda ch: pass_on(1, ch))
     y_copy(row_x, 0, r, 0).wait_recv()
@@ -364,14 +480,16 @@
     y_copy(row_d, 0, r, 4).wait_recv()
     y_copy(row_d, 1, r, 5).wait_recv()
 
+    wait_twin(0)
+
     def first(ch):
-        wait_twin(z, ch)
+        expand(twins[0], 2 * z + 1 - core, ch)
         acc[pl.ds(ch * STEP, STEP), :] = multiply(z, ch)
 
     loop(0, CHUNKS, first)
-    loop(0, CHUNKS, lambda ch: add(1, ch))
+    add(1)
     loop(2, CHUNKS, lambda ch: pass_on(2, ch))
-    loop(0, CHUNKS, lambda ch: add(2, ch))
+    add(2)
 
     eye_f = eye.astype(jnp.float32)
 
@@ -381,22 +499,15 @@
             rows = pl.ds(ch * STEP + i * BS, BS)
             for j in range(QB):
                 cols = slice(j * BS, (j + 1) * BS)
-                keep = pat[2 * QB + j, block_row].astype(jnp.float32)
+                keep = pat_p[j, block_row].astype(jnp.float32)
                 xnew = 1.5 * xg[c, rows, cols].astype(jnp.float32) - 0.5 * (acc[rows, cols] * keep)
                 sgn[rows, cols] = xnew.astype(jnp.bfloat16)
                 on = jnp.where(r * 8 + block_row == c * QB + j, 0.5, 0.0).astype(jnp.float32)
                 dens[block_row * QB + j] = (on * eye_f - 0.5 * xnew).astype(jnp.bfloat16)
 
-    pass_on(3, 0)
-
-    def last(ch):
-        pass_on(3, ch)
-        add(3, ch - 1)
-        finish(ch - 1)
-
-    loop(1, CHUNKS, last)
-    add(3, CHUNKS - 1)
-    finish(CHUNKS - 1)
+    loop(0, CHUNKS, lambda ch: pass_on(3, ch))
+    add(3)
+    loop(0, CHUNKS, finish)
 
     put = pltpu.make_async_copy(sgn, sign_hbm, local_sem.at[4])
     put.start()
@@ -411,46 +522,70 @@
             device_id_type=MESH,
         )
 
-    flips = (3 - z, (z + 2) % LINE, z + 1 - 2 * (z % 2), z)
-    for n, zz in enumerate(flips):
+    inner = z * (LINE - 1 - z) // 2
+    near = z + 1 - 2 * (z % 2)
+    far = (z + 2) % LINE
+    planes = (
+        LINE - 1 - z,
+        far + inner * (z - far),
+        near + inner * (far - near),
+        z + inner * (near - z),
+    )
+    for zz in planes:
 
         def send(j, zz=zz):
             o = (r + j // 2) % ROWS * COLS + zz * 2 + (core + j) % 2
-            for k in range(CAP):
-                outbox[o, k] = dens[table[0, o * CAP + k]]
-            d_copy(o, me).start()
-
-        loop(0 if n < 3 else 1, COLS, send)
+
+            @pl.when(o != me)
+            def _():
+                for k in range(CAP):
+                    outbox[o, k] = dens[table[o * CAP + k]]
+                d_copy(o, me).start()
+
+        loop(0, COLS, send)
 
     def force(s, block):
         parts[pl.ds(s, 1), :] = jnp.sum(block.astype(jnp.float32) * wbuf[s], axis=0, keepdims=True)
 
     for k in range(CAP):
-        force(me * CAP + k, dens[table[0, me * CAP + k]])
-
-    for n in (3, 2, 1, 0):
-
-        def take(j, zz=flips[n]):
+        force(me * CAP + k, dens[table[me * CAP + k]])
+
+    for zz in (1, 2, 0, 3):
+
+        def take(j, zz=zz):
             src = (r + ROWS - j // 2) % ROWS * COLS + zz * 2 + (core + j) % 2
-            d_copy(src, src).wait_recv()
-            for k in range(CAP):
-                force(src * CAP + k, inbox[src, k])
-
-        loop(0 if n < 3 else 1, COLS, take)
+
+            @pl.when(src != me)
+            def _():
+                d_copy(src, src).wait_recv()
+                for k in range(CAP):
+                    force(src * CAP + k, inbox[src, k])
+
+        loop(0, COLS, take)
 
     def sent(ch):
-        for zp in range(LINE):
-            panel = 2 * zp + core
-
-            @pl.when((z >= zp) & (z < LINE - 1))
-            def _():
-                up(panel, ch).wait_send()
-
-            @pl.when((z <= zp) & (z > 0))
-            def _():
-                down(panel, ch).wait_send()
-
-            twin(panel, ch).wait_send()
+        twin(0, ch).wait_send()
+        for d in range(LINE):
+
+            @pl.when(z >= d)
+            def _(d=d):
+                if d:
+                    twin(d, ch).wait_send()
+                if d < LINE - 1:
+
+                    @pl.when(z < LINE - 1)
+                    def _():
+                        up(d, ch).wait_send()
+
+            @pl.when(z + d < LINE)
+            def _(d=d):
+                if d:
+                    twin(LINE - 1 + d, ch).wait_send()
+                if d < LINE - 1:
+
+                    @pl.when(z > 0)
+                    def _():
+                        down(d, ch).wait_send()
 
     loop(0, CHUNKS, sent)
     y_copy(r, 0, row_x, 0).wait_send()
@@ -459,6 +594,8 @@
     y_copy(r, 0, row_y, 3).wait_send()
     y_copy(row_x, 0, row_y, 4).wait_send()
     y_copy(row_y, 1, row_x, 5).wait_send()
+    out = t_in.at[pl.ds(0, COLS - 1)]
+    pltpu.make_async_copy(out, out, tsend_sem).wait()
     out = e_out.at[pl.ds(0, DEVICES - 1)]
     pltpu.make_async_copy(out, out, esend_sem).wait()
     out = outbox.at[pl.ds(0, DEVICES - 1)]
@@ -467,6 +604,8 @@
 
 
 def fused(
+    room,
+    number,
     sign_iterate,
     sign_square,
     pattern_x,
@@ -479,35 +618,30 @@
     force_s,
 ):
     slots = DEVICES * CAP
-    dest = pair_dest[0, :, 0]
-    slot = dest * CAP + rank_within(dest)
-    none = sign_iterate.shape[0] // BS * QB
-    named = slot[:, None] == jnp.arange(slots, dtype=jnp.int32)[None, :]
-    table = none - jnp.sum(
-        jnp.where(named, none - pair_block[0][:, None], 0), axis=0, keepdims=True
-    )
-    pat = jnp.concatenate([pattern_x.T, pattern_y.T, pattern_product.T], axis=0)
-    energy = orbital_energy.reshape(-1, BS).astype(jnp.float32)
-    energy = jnp.concatenate([energy, jnp.zeros_like(energy)], axis=0)
+    blocks = QB * TALL
     vmem = pl.BlockSpec(memory_space=pltpu.VMEM)
     smem = pl.BlockSpec(memory_space=pltpu.SMEM)
     hbm = pl.BlockSpec(memory_space=pl.ANY)
-    bf16, f32 = jnp.bfloat16, jnp.float32
+    bf16, f32, i32 = jnp.bfloat16, jnp.float32, jnp.int32
     dma = pltpu.SemaphoreType.DMA
-    sign_next, parts = pl.pallas_call(
-        kernel,
+    tile = sign_iterate.shape
+    return pl.pallas_call(
+        functools.partial(kernel, room),
         out_shape=(
-            jax.ShapeDtypeStruct(sign_iterate.shape, bf16),
-            jax.ShapeDtypeStruct((slots, BS), f32),
+            jax.ShapeDtypeStruct(tile, bf16),
+            jax.ShapeDtypeStruct((slots + 8, BS), f32),
         ),
-        in_specs=[smem, smem, vmem, hbm, hbm, hbm, hbm],
+        in_specs=[smem] * 5 + [vmem] * 2 + [hbm] * 4,
         out_specs=(hbm, vmem),
         scratch_shapes=[
-            pltpu.VMEM((COLS, 1024, 512), bf16),
-            pltpu.VMEM((ROWS, 1024, 512), bf16),
-            pltpu.VMEM((1024, 512), f32),
-            pltpu.VMEM((none + 1, BS, BS), bf16),
-            pltpu.VMEM((1024, 512), bf16),
+            pltpu.VMEM((blocks, BS, BS), bf16),
+            [pltpu.VMEM((blocks + 1, BS, BS), bf16)] * (2 * LINE - 1),
+            [pltpu.VMEM((blocks + 1, BS, BS), bf16)] * (2 * LINE - 1),
+            pltpu.VMEM((COLS, *tile), bf16),
+            pltpu.VMEM((ROWS, *tile), bf16),
+            pltpu.VMEM(tile, f32),
+            pltpu.VMEM((blocks + 1, BS, BS), bf16),
+            pltpu.VMEM(tile, bf16),
             pltpu.VMEM((slots, BS, BS), bf16),
             pltpu.VMEM((slots, BS, BS), bf16),
             pltpu.VMEM((slots, BS, BS), f32),
@@ -515,26 +649,61 @@
             pltpu.VMEM((DEVICES, CAP, BS, BS), bf16),
             pltpu.VMEM((DEVICES, 8, BS), f32),
             pltpu.VMEM((DEVICES, 8, BS), f32),
-            dma((5,)),
-            dma((LINE, CHUNKS)),
-            dma((LINE, CHUNKS)),
-            dma((LINE, CHUNKS)),
-            dma((COLS, CHUNKS)),
+            pltpu.VMEM((2 * TALL, BS), f32),
+            pltpu.VMEM((8, BS), i32),
+            pltpu.VMEM((COLS, 8, BS), i32),
+            pltpu.SMEM((COLS, 8, BS), i32),
+            pltpu.SMEM((blocks,), i32),
+            pltpu.SMEM((blocks,), i32),
+            pltpu.SMEM((COLS, blocks), i32),
+            pltpu.SMEM((slots,), i32),
+            dma((6,)),
+            dma((LINE - 1, CHUNKS)),
+            dma((LINE - 1, CHUNKS)),
+            dma((2 * LINE - 1, CHUNKS)),
+            dma((2 * LINE - 1, CHUNKS)),
+            dma((2 * LINE - 1, CHUNKS)),
             dma((6,)),
             dma((ROWS, 2)),
             dma,
             dma,
             dma((DEVICES,)),
             dma,
+            dma,
+            dma,
         ],
         compiler_params=pltpu.CompilerParams(
-            collective_id=0, has_side_effects=True, vmem_limit_bytes=48 * 1024 * 1024
+            collective_id=number, has_side_effects=True, vmem_limit_bytes=60 * 1024 * 1024
         ),
         cost_estimate=pl.CostEstimate(
             flops=2 * 1024 * 4096 * 512, bytes_accessed=8 * 1024 * 1024, transcendentals=0
         ),
-    )(pat, table, energy, sign_iterate, sign_square, force_h, force_s)
-    return sign_next, jnp.sum(parts, axis=1)
+        name=f"room_{room}",
+    )(
+        pattern_x.T,
+        pattern_y.T,
+        pattern_product.T,
+        pair_dest[:, :, 0],
+        pair_block,
+        pattern_x.T,
+        orbital_energy.reshape(-1, BS),
+        sign_iterate.reshape(TALL, BS, tile[1]),
+        sign_square,
+        force_h,
+        force_s,
+    )
+
+
+ROOM = 24
+
+
+def adaptive(*arrays):
+    sign_next, parts = fused(ROOM, 0, *arrays)
+    short = parts[DEVICES * CAP, 0] > ROOM
+    sign_next, parts = lax.cond(
+        short, lambda: tuple(fused(QB * TALL, 1, *arrays)), lambda: (sign_next, parts)
+    )
+    return sign_next, jnp.sum(parts[: DEVICES * CAP], axis=1)
 
 
 def solution(mesh):
@@ -551,5 +720,5 @@
         P(("row", "col"), None, None),
     )
     out_specs = (P("row", "col"), P(("row", "col")))
-    body = fused if (mesh.shape["row"], mesh.shape["col"]) == (ROWS, COLS) else shards
+    body = adaptive if (mesh.shape["row"], mesh.shape["col"]) == (ROWS, COLS) else shards
     return jax.shard_map(body, mesh=mesh, in_specs=in_specs, out_specs=out_specs, check_vma=False)

time: 147 us -> 120 us (0.82)
  Pallas kernels: 136 us -> 115 us
  other arithmetic: 4.36 us -> 0.62 us
  local copies, waits for them, and re-layouts: 5.01 us -> 1.51 us
    pallas_call x1, Pallas kernels: 136 us -> 115 us  [fused(): pl.pallas_call(functools.partial(kernel, room), out_shape=(jax.ShapeDtype...]
    unnamed x7 -> x15, local copies, waits for them, and re-layouts: 5.01 us -> 1 us
where the time goes in v2:
time: 120 us; the launch traced here: 119 us
  Pallas kernels  115 us (96%)
  local copies, waits for them, and re-layouts  1.51 us (1%)
  between operations  1.41 us (1%)
    pallas_call x1, Pallas kernels, fused(): pl.pallas_call(functools.partial(kernel, room), out_shape=(jax.ShapeDtype...  115 us

profile of v2, /device:TPU:1, one launch (start us, length us, event | category | flops | bytes accessed | tf_op | source)
XLA Modules:
  0.0 118.9 jit_solution(13965833920822187850)
XLA Ops:
  0.6 0.0 copy-start
  0.6 0.0 copy-start.1
  0.7 0.0 copy-start.2
  0.7 0.0 copy-start.3
  0.7 0.0 copy-start.4
  0.7 0.0 copy-start.5
  0.7 0.0 copy-start.6
  0.7 115.3 %room_24.1 = (bf16[1024,512]{1,0:T(8,128)(2,1)S(1)}, f32[72,128]{1,0:T(8,128)S(1)}) custom-call(s32[4,8]{1,0:T(4,128)} %bitcast.15, s32[4,8]{1,0:T(4,128)} %bitcast.19, s32[4,8]{1,0:T(4,128)} %bitcast.21, s32[1,32]{1,0:T(1,128)} %bitcast.25, s32[1,32]{1,0:T(1,128)} %wanted.1, s32[4,8]{1,0:T(4,128)} %bitcast.16, bf16[8,128]{1,0:T(8,128)(2,1)} %bitcast.23, ...), custom_call_target="tpu_custom_call" | custom-call | flops 4294967296 | bytes 8388608 | tf_op jit(solution)/shard_map/room_24/pallas_call | solution.py:628
  116.0 0.5 slice.10
  117.2 0.0 copy-done
  117.2 0.0 copy-done.1
  117.2 0.0 copy-done.2
  117.2 0.0 copy-done.3
  117.2 0.0 copy-done.4
  117.2 0.0 copy-done.5
  117.3 0.0 copy-done.6
  117.3 0.6 slice_reduce_fusion
  117.9 1.0 copy.17
  (1 shorter events, 0.0 us)
Async XLA Ops:
  0.6 116.6 %copy-start = (bf16[64,128,128]{2,1,0:T(8,128)(2,1)S(1)}, bf16[64,128,128]{2,1,0:T(8,128)(2,1)}, u32[]{:S(2)}) copy-start(bf16[64,128,128]{2,1,0:T(8,128)(2,1)} %h_hbm.1) | copy-start | bytes 6291460
  0.6 116.6 %copy-start.1 = (s32[8,4]{0,1:T(4,128)S(1)}, s32[8,4]{0,1:T(4,128)}, u32[]{:S(2)}) copy-start(s32[8,4]{0,1:T(4,128)} %param.14) | copy-start | bytes 388
  0.7 116.6 %copy-start.2 = (s32[8,4]{0,1:T(4,128)S(1)}, s32[8,4]{0,1:T(4,128)}, u32[]{:S(2)}) copy-start(s32[8,4]{0,1:T(4,128)} %param.15) | copy-start | bytes 388
  0.7 116.6 %copy-start.3 = (s32[8,4]{0,1:T(4,128)S(1)}, s32[8,4]{0,1:T(4,128)}, u32[]{:S(2)}) copy-start(s32[8,4]{0,1:T(4,128)} %param.16) | copy-start | bytes 388
  0.7 116.6 %copy-start.4 = (bf16[1024]{0:T(1024)(128)(2,1)S(1)}, bf16[1024]{0:T(1024)(128)(2,1)}, u32[]{:S(2)}) copy-start(bf16[1024]{0:T(1024)(128)(2,1)} %param.17) | copy-start | bytes 6148
  0.7 116.6 %copy-start.5 = (s32[1,32,1]{1,2,0:T(1,128)S(1)}, s32[1,32,1]{1,2,0:T(1,128)}, u32[]{:S(2)}) copy-start(s32[1,32,1]{1,2,0:T(1,128)} %param.18) | copy-start | bytes 388
  0.7 116.6 %copy-start.6 = (s32[1,32]{1,0:T(1,128)S(1)}, s32[1,32]{1,0:T(1,128)}, u32[]{:S(2)}) copy-start(s32[1,32]{1,0:T(1,128)} %wanted.1) | copy-start | bytes 388

commit v3 on v2

--- a/solution.py
+++ b/solution.py
@@ -116,6 +116,8 @@
 CHUNKS = 4
 TALL = 8
 STEP = 256
+PIECES = 2
+KEPT = 16
 HALF = 512
 
 
@@ -134,9 +136,11 @@
     s_hbm,
     sign_hbm,
     parts,
+    short,
     xraw,
     lines,
-    twins,
+    spill_out,
+    spill_in,
     xg,
     yg,
     acc,
@@ -149,6 +153,7 @@
     inbox,
     e_out,
     e_in,
+    e_table,
     e_rows,
     t_out,
     t_in,
@@ -156,6 +161,7 @@
     ahead,
     listed,
     place,
+    tallies,
     table,
     local_sem,
     up_sem,
@@ -171,8 +177,13 @@
     dsend_sem,
     t_sem,
     tsend_sem,
+    spill_sem,
+    rows_sem,
+    rsend_sem,
 ):
-    chunk = room // CHUNKS
+    blocks = QB * TALL
+    piece = room // PIECES
+    spill = blocks - room
     r = lax.axis_index("row")
     c = lax.axis_index("col")
     me = r * COLS + c
@@ -198,7 +209,8 @@
             xraw.at[pl.ds(j * TALL, TALL)],
             local_sem.at[0],
         ).start()
-    get_x = pltpu.make_async_copy(xraw, xraw, local_sem.at[0])
+    whole = xraw.at[pl.ds(0, blocks)]
+    get_x = pltpu.make_async_copy(whole, whole, local_sem.at[0])
     get_y = pltpu.make_async_copy(y_hbm, yg.at[r], local_sem.at[1])
     get_h = pltpu.make_async_copy(h_hbm, hbuf, local_sem.at[2])
     get_s = pltpu.make_async_copy(s_hbm, sbuf, local_sem.at[3])
@@ -213,11 +225,13 @@
 
         lax.fori_loop(lo, hi, step, 0)
 
+    half = blocks + 1
+
     def x_copy(src, dst, ch, col, send_sem, recv_sem):
-        rows = pl.ds(ch * chunk, chunk)
+        rows = pl.ds(core * half + ch * piece, piece)
         return pltpu.make_async_remote_copy(
-            src_ref=src.at[rows],
-            dst_ref=dst.at[rows],
+            src_ref=lines[src].at[rows],
+            dst_ref=lines[dst].at[rows],
             send_sem=send_sem,
             recv_sem=recv_sem,
             device_id=(r, col),
@@ -225,16 +239,21 @@
         )
 
     def up(d, ch):
-        return x_copy(lines[d], lines[d + 1], ch, c + 2, up_sem.at[d, ch], x_sem.at[d + 1, ch])
+        return x_copy(d, d + 1, ch, c + 2, up_sem.at[d, ch], x_sem.at[d + 1, ch])
 
     def down(d, ch):
-        src = lines[d + LINE - 1] if d else lines[0]
         to = d + LINE
-        return x_copy(src, lines[to], ch, c - 2, down_sem.at[d, ch], x_sem.at[to, ch])
+        src = to - 1 if d else 0
+        return x_copy(src, to, ch, c - 2, down_sem.at[d, ch], x_sem.at[to, ch])
+
+    twin_col = c + 1 - 2 * core
 
     def twin(i, ch):
-        other = c + 1 - 2 * core
-        return x_copy(lines[i], twins[i], ch, other, twin_sem.at[i, ch], tx_sem.at[i, ch])
+        return x_copy(i, i, ch, twin_col, twin_sem.at[i, ch], tx_sem.at[i, ch])
+
+    def from_twin(i, ch):
+        rows = pl.ds((1 - core) * half + ch * piece, piece)
+        return pltpu.make_async_copy(lines[i].at[rows], lines[i].at[rows], tx_sem.at[i, ch])
 
     def y_copy(owner, half, to, number):
         block = yg.at[owner, pl.ds(half * HALF, HALF)]
@@ -249,30 +268,36 @@
 
     t_out[...] = jnp.zeros_like(t_out)
     t_out[0:QB, 0:TALL] = pat_tile[...]
-    blocks = QB * TALL
     number = jnp.int32(0)
-    spots = []
     for b in range(blocks):
-        on = pat_x[b // TALL, b % TALL]
-        spots.append(on * number + (1 - on) * blocks)
-        number = number + on
+        number = number + pat_x[b // TALL, b % TALL]
+        ahead[b] = number
     count = number
-    for b in range(blocks):
-        ahead[b] = spots[b]
 
     def seek(t):
         found = jnp.int32(0)
         for b in range(blocks):
-            found = found + (ahead[b] == t).astype(jnp.int32) * b
+            found = found + (ahead[b] <= t).astype(jnp.int32)
         listed[t] = found
 
-    loop(0, room, seek)
+    loop(0, blocks, seek)
+    xraw[blocks] = jnp.zeros((BS, BS), jnp.bfloat16)
+
+    def at_least(n, low):
+        return low + (n > low).astype(jnp.int32) * (n - low)
+
     get_x.wait()
 
+    early = KEPT if spill else room
+
     def compact(t):
-        lines[0][t] = xraw[listed[t]]
-
-    loop(0, room, compact)
+        lines[0][core * half + t] = xraw[listed[t]]
+
+    loop(0, early, compact)
+    for t in range(spill):
+        spill_out[t] = xraw[listed[room + t]]
+    if spill:
+        spill_in[spill] = jnp.zeros((BS, BS), jnp.bfloat16)
     pl.semaphore_wait(barrier, DEVICES - 1)
 
     def t_copy(col):
@@ -299,7 +324,29 @@
 
         twin(0, ch).start()
 
-    loop(0, CHUNKS, send_x)
+    hand_over = None
+    if spill:
+        hand_over = pltpu.make_async_remote_copy(
+            src_ref=spill_out,
+            dst_ref=spill_in.at[pl.ds(0, spill)],
+            send_sem=spill_sem.at[0],
+            recv_sem=spill_sem.at[1],
+            device_id=(r, twin_col),
+            device_id_type=MESH,
+        )
+        hand_over.start()
+    send_x(0)
+    if spill:
+        hand_over.wait_recv()
+        used = at_least(count, KEPT)
+
+        def fill(t):
+            own = (t < count).astype(jnp.int32)
+            extra = spill_in[own * spill + (1 - own) * (t - used) * (t >= used).astype(jnp.int32)]
+            lines[0][core * half + t] = xraw[listed[t]] + extra
+
+        loop(early, room, fill)
+    loop(1, PIECES, send_x)
     get_y.wait()
 
     def mask_y(i):
@@ -337,17 +384,15 @@
             table[o * CAP + k] = slots[k]
 
     loop(0, DEVICES, find)
-    e_rows[0:TALL, :] = energy[...].astype(jnp.float32)
-    e_rows[TALL : 2 * TALL, :] = jnp.zeros((TALL, BS), jnp.float32)
-
-    def pack_energy(o, carry):
+    lanes = lax.broadcasted_iota(jnp.int32, (1, BS), 1)
+
+    def pack(o):
+        line = jnp.full((1, BS), count)
         for k in range(CAP):
-            e_out[o, k : k + 1, :] = e_rows[pl.ds(table[o * CAP + k] // QB, 1), :]
-        for k in range(CAP, 8):
-            e_out[o, k : k + 1, :] = jnp.full((1, BS), count.astype(jnp.float32))
-        return carry
-
-    lax.fori_loop(0, DEVICES, pack_energy, 0)
+            line = jnp.where(lanes == k, table[o * CAP + k], line)
+        e_out[o] = line
+
+    loop(0, DEVICES, pack)
 
     def e_copy(o):
         return pltpu.make_async_remote_copy(
@@ -359,17 +404,41 @@
             device_id_type=MESH,
         )
 
-    def send_energy(i, carry):
-        e_copy((me + i) % DEVICES).start()
-        return carry
-
-    lax.fori_loop(1, DEVICES, send_energy, 0)
+    loop(1, DEVICES, lambda i: e_copy((me + i) % DEVICES).start())
     pltpu.make_async_copy(e_out.at[me], e_in.at[me], e_sem).start()
+
+    for i in range(ROWS):
+        e_rows[i, TALL : 2 * TALL, :] = jnp.zeros((TALL, BS), jnp.float32)
+    own_rows = e_rows.at[r, pl.ds(0, TALL)]
+    own_rows[...] = energy[...].astype(jnp.float32)
+
+    def row_copy(i):
+        return pltpu.make_async_remote_copy(
+            src_ref=own_rows,
+            dst_ref=own_rows,
+            send_sem=rsend_sem.at[i],
+            recv_sem=rows_sem.at[r],
+            device_id=((r + i) % ROWS, c),
+            device_id_type=MESH,
+        )
+
+    def row_arrival(i):
+        other = (r + i) % ROWS
+        ref = e_rows.at[other, pl.ds(0, TALL)]
+        return pltpu.make_async_copy(ref, ref, rows_sem.at[other])
+
+    for i in range(1, ROWS):
+        row_copy(i).start()
 
     dens[QB * 8] = jnp.zeros((BS, BS), jnp.bfloat16)
     get_h.wait()
     get_s.wait()
     pltpu.make_async_copy(e_in, e_in, e_sem).wait()
+    get_table = pltpu.make_async_copy(e_in, e_table, local_sem.at[5])
+    get_table.start()
+    get_table.wait()
+    for i in range(1, ROWS):
+        row_arrival(i).wait()
 
     eye = lax.broadcasted_iota(jnp.int32, (BS, BS), 0) == lax.broadcasted_iota(
         jnp.int32, (BS, BS), 1
@@ -377,7 +446,8 @@
 
     def weigh(src, carry):
         for k in range(CAP):
-            line = jnp.broadcast_to(e_in[src, k : k + 1, :], (BS, BS))
+            line = e_rows[src // COLS, pl.ds(e_table[src, 0, k] // QB, 1), :]
+            line = jnp.broadcast_to(line, (BS, BS))
             col = jnp.sum(jnp.where(eye, line, 0.0), axis=1, keepdims=True)
             s = src * CAP + k
             wbuf[s] = hbuf[s].astype(jnp.float32) - col * sbuf[s].astype(jnp.float32)
@@ -385,24 +455,44 @@
 
     lax.fori_loop(0, DEVICES, weigh, 0)
 
-    most = e_in[0]
-    for src in range(1, DEVICES):
-        most = jnp.maximum(most, e_in[src])
-    parts[DEVICES * CAP : DEVICES * CAP + 8, :] = jnp.broadcast_to(most[CAP : CAP + 1, :], (8, BS))
+    wrong = jnp.int32(0)
+    for src in range(DEVICES):
+        mine, other = e_table[src, 0, CAP], e_table[src + 1 - 2 * (src % 2), 0, CAP]
+        over = (mine > room).astype(jnp.int32) * (mine - room)
+        free = (other < room).astype(jnp.int32) * (room - at_least(other, KEPT))
+        wrong = wrong + (over > free).astype(jnp.int32)
+    short[0] = (wrong > 0).astype(jnp.int32)
 
     pltpu.make_async_copy(t_in, t_in, t_sem).wait()
     get_pats = pltpu.make_async_copy(t_in, pats, local_sem.at[5])
     get_pats.start()
     get_pats.wait()
 
-    for ref in (*lines, *twins):
+    for ref in lines:
         ref[blocks] = jnp.zeros((BS, BS), jnp.bfloat16)
+        ref[half + blocks] = jnp.zeros((BS, BS), jnp.bfloat16)
+
+    def tally(panel):
+        number = jnp.int32(0)
+        for b in range(blocks):
+            number = number + pats[panel, b // TALL, b % TALL]
+        tallies[panel] = number
+
+    loop(0, COLS, tally)
 
     def locate(panel):
+        kind = panel % 2
+        start = kind * half
+        beyond = (1 - kind) * half + at_least(tallies[panel + 1 - 2 * kind], KEPT)
+        last_spot = (1 - kind) * half + blocks
         number = jnp.int32(0)
         for b in range(blocks):
             on = pats[panel, b // TALL, b % TALL]
-            place[panel, b] = on * number + (1 - on) * blocks
+            fits = (number < room).astype(jnp.int32)
+            past = beyond + number - room
+            past = past - (past > last_spot).astype(jnp.int32) * (past - last_spot)
+            spot = fits * (start + number) + (1 - fits) * past
+            place[panel, b] = on * spot + (1 - on) * blocks
             number = number + on
 
     loop(0, COLS, locate)
@@ -431,7 +521,7 @@
             twin(LINE - 1 + d, ch).start()
 
     def wait_twin(i):
-        loop(0, CHUNKS, lambda ch: twin(i, ch).wait_recv())
+        loop(0, PIECES, lambda ch: from_twin(i, ch).wait())
 
     def expand(ref, panel, ch):
         for i in range(STEP // BS):
@@ -453,8 +543,8 @@
             wait_twin(i)
 
             def one(ch):
-                expand(lines[i], 2 * zp + core, ch)
-                expand(twins[i], 2 * zp + 1 - core, ch)
+                expand(lines[i], 2 * zp, ch)
+                expand(lines[i], 2 * zp + 1, ch)
                 acc[pl.ds(ch * STEP, STEP), :] += multiply(zp, ch)
 
             loop(0, CHUNKS, one)
@@ -467,28 +557,27 @@
         def _():
             panels(z + d, LINE - 1 + d)
 
-    loop(0, 2, lambda ch: pass_on(1, ch))
+    loop(0, 1, lambda ch: pass_on(1, ch))
     y_copy(row_x, 0, r, 0).wait_recv()
     y_copy(row_x, 0, row_y, 4).start()
     y_copy(row_y, 1, r, 1).wait_recv()
     y_copy(row_y, 1, row_x, 5).start()
-    loop(2, CHUNKS, lambda ch: pass_on(1, ch))
-    loop(0, 2, lambda ch: pass_on(2, ch))
+    loop(1, PIECES, lambda ch: pass_on(1, ch))
+    loop(0, 1, lambda ch: pass_on(2, ch))
     y_copy(row_x, 1, r, 2).wait_recv()
     y_copy(row_y, 0, r, 3).wait_recv()
     row_d = 3 - r
     y_copy(row_d, 0, r, 4).wait_recv()
     y_copy(row_d, 1, r, 5).wait_recv()
-
     wait_twin(0)
 
     def first(ch):
-        expand(twins[0], 2 * z + 1 - core, ch)
+        expand(lines[0], 2 * z + 1 - core, ch)
         acc[pl.ds(ch * STEP, STEP), :] = multiply(z, ch)
 
     loop(0, CHUNKS, first)
     add(1)
-    loop(2, CHUNKS, lambda ch: pass_on(2, ch))
+    loop(1, PIECES, lambda ch: pass_on(2, ch))
     add(2)
 
     eye_f = eye.astype(jnp.float32)
@@ -505,7 +594,7 @@
                 on = jnp.where(r * 8 + block_row == c * QB + j, 0.5, 0.0).astype(jnp.float32)
                 dens[block_row * QB + j] = (on * eye_f - 0.5 * xnew).astype(jnp.bfloat16)
 
-    loop(0, CHUNKS, lambda ch: pass_on(3, ch))
+    loop(0, PIECES, lambda ch: pass_on(3, ch))
     add(3)
     loop(0, CHUNKS, finish)
 
@@ -587,7 +676,11 @@
                     def _():
                         down(d, ch).wait_send()
 
-    loop(0, CHUNKS, sent)
+    loop(0, PIECES, sent)
+    if spill:
+        hand_over.wait_send()
+    for i in range(1, ROWS):
+        row_copy(i).wait_send()
     y_copy(r, 0, row_x, 0).wait_send()
     y_copy(r, 1, row_y, 1).wait_send()
     y_copy(r, 1, row_x, 2).wait_send()
@@ -629,14 +722,16 @@
         functools.partial(kernel, room),
         out_shape=(
             jax.ShapeDtypeStruct(tile, bf16),
-            jax.ShapeDtypeStruct((slots + 8, BS), f32),
+            jax.ShapeDtypeStruct((slots, BS), f32),
+            jax.ShapeDtypeStruct((1,), i32),
         ),
         in_specs=[smem] * 5 + [vmem] * 2 + [hbm] * 4,
-        out_specs=(hbm, vmem),
+        out_specs=(hbm, vmem, smem),
         scratch_shapes=[
-            pltpu.VMEM((blocks, BS, BS), bf16),
-            [pltpu.VMEM((blocks + 1, BS, BS), bf16)] * (2 * LINE - 1),
-            [pltpu.VMEM((blocks + 1, BS, BS), bf16)] * (2 * LINE - 1),
+            pltpu.VMEM((blocks + 1, BS, BS), bf16),
+            [pltpu.VMEM((2 * blocks + 2, BS, BS), bf16)] * (2 * LINE - 1),
+            pltpu.VMEM((max(blocks - room, 1), BS, BS), bf16),
+            pltpu.VMEM((blocks - room + 1, BS, BS), bf16),
             pltpu.VMEM((COLS, *tile), bf16),
             pltpu.VMEM((ROWS, *tile), bf16),
             pltpu.VMEM(tile, f32),
@@ -647,22 +742,24 @@
             pltpu.VMEM((slots, BS, BS), f32),
             pltpu.VMEM((DEVICES, CAP, BS, BS), bf16),
             pltpu.VMEM((DEVICES, CAP, BS, BS), bf16),
-            pltpu.VMEM((DEVICES, 8, BS), f32),
-            pltpu.VMEM((DEVICES, 8, BS), f32),
-            pltpu.VMEM((2 * TALL, BS), f32),
-            pltpu.VMEM((8, BS), i32),
-            pltpu.VMEM((COLS, 8, BS), i32),
-            pltpu.SMEM((COLS, 8, BS), i32),
+            pltpu.VMEM((DEVICES, 1, BS), i32),
+            pltpu.VMEM((DEVICES, 1, BS), i32),
+            pltpu.SMEM((DEVICES, 1, BS), i32),
+            pltpu.VMEM((ROWS, 2 * TALL, BS), f32),
+            pltpu.VMEM((QB, BS), i32),
+            pltpu.VMEM((COLS, QB, BS), i32),
+            pltpu.SMEM((COLS, QB, BS), i32),
             pltpu.SMEM((blocks,), i32),
             pltpu.SMEM((blocks,), i32),
             pltpu.SMEM((COLS, blocks), i32),
+            pltpu.SMEM((COLS,), i32),
             pltpu.SMEM((slots,), i32),
             dma((6,)),
-            dma((LINE - 1, CHUNKS)),
-            dma((LINE - 1, CHUNKS)),
-            dma((2 * LINE - 1, CHUNKS)),
-            dma((2 * LINE - 1, CHUNKS)),
-            dma((2 * LINE - 1, CHUNKS)),
+            dma((LINE - 1, PIECES)),
+            dma((LINE - 1, PIECES)),
+            dma((2 * LINE - 1, PIECES)),
+            dma((2 * LINE - 1, PIECES)),
+            dma((2 * LINE - 1, PIECES)),
             dma((6,)),
             dma((ROWS, 2)),
             dma,
@@ -671,6 +768,9 @@
             dma,
             dma,
             dma,
+            dma((2,)),
+            dma((ROWS,)),
+            dma((ROWS,)),
         ],
         compiler_params=pltpu.CompilerParams(
             collective_id=number, has_side_effects=True, vmem_limit_bytes=60 * 1024 * 1024
@@ -694,16 +794,16 @@
     )
 
 
-ROOM = 24
+ROOM = 22
 
 
 def adaptive(*arrays):
-    sign_next, parts = fused(ROOM, 0, *arrays)
-    short = parts[DEVICES * CAP, 0] > ROOM
-    sign_next, parts = lax.cond(
-        short, lambda: tuple(fused(QB * TALL, 1, *arrays)), lambda: (sign_next, parts)
-    )
-    return sign_next, jnp.sum(parts[: DEVICES * CAP], axis=1)
+    sign_next, parts, short = fused(ROOM, 0, *arrays)
+    sign_next, parts = lax.switch(
+        short[0],
+        (lambda: (sign_next, parts), lambda: tuple(fused(QB * TALL, 1, *arrays)[:2])),
+    )
+    return sign_next, jnp.sum(parts, axis=1)
 
 
 def solution(mesh):

time: 120 us -> 119 us (level)
  no operation moved by 1% of the time
where the time goes in v3:
time: 119 us; the launch traced here: 118 us
  Pallas kernels  115 us (97%)
  between operations  1.39 us (1%)
    pallas_call x1, Pallas kernels, fused(): pl.pallas_call(functools.partial(kernel, room), out_shape=(jax.ShapeDtype...  115 us

profile of v3, /device:TPU:1, one launch (start us, length us, event | category | flops | bytes accessed | tf_op | source)
XLA Modules:
  0.0 117.9 jit_solution(3442597430730064108)
XLA Ops:
  0.6 0.0 copy-start
  0.6 0.0 copy-start.1
  0.7 0.0 copy-start.2
  0.7 0.0 copy-start.3
  0.7 0.0 copy-start.4
  0.7 0.0 copy-start.5
  0.7 0.0 copy-start.6
  0.7 114.8 %room_22.1 = (bf16[1024,512]{1,0:T(8,128)(2,1)S(1)}, f32[64,128]{1,0:T(8,128)S(1)}, s32[1]{0:T(128)}) custom-call(s32[4,8]{1,0:T(4,128)} %bitcast.15, s32[4,8]{1,0:T(4,128)} %bitcast.19, s32[4,8]{1,0:T(4,128)} %bitcast.21, s32[1,32]{1,0:T(1,128)} %bitcast.25, s32[1,32]{1,0:T(1,128)} %wanted.1, s32[4,8]{1,0:T(4,128)} %bitcast.16, bf16[8,128]{1,0:T(8,128)(2,1)} %bitcast.23, ...), custom_call_target="tpu_custom_call" | custom-call | flops 4294967296 | bytes 8388608 | tf_op jit(solution)/shard_map/room_22/pallas_call | solution.py:721
  116.2 0.0 copy-done
  116.2 0.0 copy-done.1
  116.2 0.0 copy-done.2
  116.2 0.0 copy-done.3
  116.2 0.0 copy-done.4
  116.2 0.0 copy-done.5
  116.2 0.0 copy-done.6
  116.3 0.6 reduce_sum.16
  116.9 1.0 copy.17
  (1 shorter events, 0.0 us)
Async XLA Ops:
  0.6 115.5 %copy-start = (bf16[64,128,128]{2,1,0:T(8,128)(2,1)S(1)}, bf16[64,128,128]{2,1,0:T(8,128)(2,1)}, u32[]{:S(2)}) copy-start(bf16[64,128,128]{2,1,0:T(8,128)(2,1)} %h_hbm.1) | copy-start | bytes 6291460
  0.6 115.5 %copy-start.1 = (s32[8,4]{0,1:T(4,128)S(1)}, s32[8,4]{0,1:T(4,128)}, u32[]{:S(2)}) copy-start(s32[8,4]{0,1:T(4,128)} %param.14) | copy-start | bytes 388
  0.7 115.5 %copy-start.2 = (s32[8,4]{0,1:T(4,128)S(1)}, s32[8,4]{0,1:T(4,128)}, u32[]{:S(2)}) copy-start(s32[8,4]{0,1:T(4,128)} %param.15) | copy-start | bytes 388
  0.7 115.5 %copy-start.3 = (s32[8,4]{0,1:T(4,128)S(1)}, s32[8,4]{0,1:T(4,128)}, u32[]{:S(2)}) copy-start(s32[8,4]{0,1:T(4,128)} %param.16) | copy-start | bytes 388
  0.7 115.5 %copy-start.4 = (bf16[1024]{0:T(1024)(128)(2,1)S(1)}, bf16[1024]{0:T(1024)(128)(2,1)}, u32[]{:S(2)}) copy-start(bf16[1024]{0:T(1024)(128)(2,1)} %param.17) | copy-start | bytes 6148
  0.7 115.5 %copy-start.5 = (s32[1,32,1]{1,2,0:T(1,128)S(1)}, s32[1,32,1]{1,2,0:T(1,128)}, u32[]{:S(2)}) copy-start(s32[1,32,1]{1,2,0:T(1,128)} %param.18) | copy-start | bytes 388
  0.7 115.5 %copy-start.6 = (s32[1,32]{1,0:T(1,128)S(1)}, s32[1,32]{1,0:T(1,128)}, u32[]{:S(2)}) copy-start(s32[1,32]{1,0:T(1,128)} %wanted.1) | copy-start | bytes 388

commit v4 on v3

--- a/solution.py
+++ b/solution.py
@@ -611,6 +611,30 @@
             device_id_type=MESH,
         )
 
+    def sent(ch):
+        twin(0, ch).wait_send()
+        for d in range(LINE):
+
+            @pl.when(z >= d)
+            def _(d=d):
+                if d:
+                    twin(d, ch).wait_send()
+                if d < LINE - 1:
+
+                    @pl.when(z < LINE - 1)
+                    def _():
+                        up(d, ch).wait_send()
+
+            @pl.when(z + d < LINE)
+            def _(d=d):
+                if d:
+                    twin(LINE - 1 + d, ch).wait_send()
+                if d < LINE - 1:
+
+                    @pl.when(z > 0)
+                    def _():
+                        down(d, ch).wait_send()
+
     inner = z * (LINE - 1 - z) // 2
     near = z + 1 - 2 * (z % 2)
     far = (z + 2) % LINE
@@ -620,7 +644,9 @@
         near + inner * (far - near),
         z + inner * (near - z),
     )
-    for zz in planes:
+    for n, zz in enumerate(planes):
+        if n == 2:
+            loop(0, PIECES, sent)
 
         def send(j, zz=zz):
             o = (r + j // 2) % ROWS * COLS + zz * 2 + (core + j) % 2
@@ -652,31 +678,6 @@
 
         loop(0, COLS, take)
 
-    def sent(ch):
-        twin(0, ch).wait_send()
-        for d in range(LINE):
-
-            @pl.when(z >= d)
-            def _(d=d):
-                if d:
-                    twin(d, ch).wait_send()
-                if d < LINE - 1:
-
-                    @pl.when(z < LINE - 1)
-                    def _():
-                        up(d, ch).wait_send()
-
-            @pl.when(z + d < LINE)
-            def _(d=d):
-                if d:
-                    twin(LINE - 1 + d, ch).wait_send()
-                if d < LINE - 1:
-
-                    @pl.when(z > 0)
-                    def _():
-                        down(d, ch).wait_send()
-
-    loop(0, PIECES, sent)
     if spill:
         hand_over.wait_send()
     for i in range(1, ROWS):

time: 119 us -> 119 us (level)
  no operation moved by 1% of the time
where the time goes in v4:
time: 119 us; the launch traced here: 118 us
  Pallas kernels  115 us (97%)
  between operations  1.39 us (1%)
    pallas_call x1, Pallas kernels, fused(): pl.pallas_call(functools.partial(kernel, room), out_shape=(jax.ShapeDtype...  115 us

profile of v4, /device:TPU:1, one launch (start us, length us, event | category | flops | bytes accessed | tf_op | source)
XLA Modules:
  0.0 118.4 jit_solution(3821632213233767413)
XLA Ops:
  0.6 0.0 copy-start
  0.6 0.0 copy-start.1
  0.7 0.0 copy-start.2
  0.7 0.0 copy-start.3
  0.7 0.0 copy-start.4
  0.7 0.0 copy-start.5
  0.7 0.0 copy-start.6
  0.7 115.4 %room_22.1 = (bf16[1024,512]{1,0:T(8,128)(2,1)S(1)}, f32[64,128]{1,0:T(8,128)S(1)}, s32[1]{0:T(128)}) custom-call(s32[4,8]{1,0:T(4,128)} %bitcast.15, s32[4,8]{1,0:T(4,128)} %bitcast.19, s32[4,8]{1,0:T(4,128)} %bitcast.21, s32[1,32]{1,0:T(1,128)} %bitcast.25, s32[1,32]{1,0:T(1,128)} %wanted.1, s32[4,8]{1,0:T(4,128)} %bitcast.16, bf16[8,128]{1,0:T(8,128)(2,1)} %bitcast.23, ...), custom_call_target="tpu_custom_call" | custom-call | flops 4294967296 | bytes 8388608 | tf_op jit(solution)/shard_map/room_22/pallas_call | solution.py:722
  116.7 0.0 copy-done
  116.7 0.0 copy-done.1
  116.7 0.0 copy-done.2
  116.7 0.0 copy-done.3
  116.7 0.0 copy-done.4
  116.7 0.0 copy-done.5
  116.8 0.0 copy-done.6
  116.8 0.6 reduce_sum.16
  117.4 1.0 copy.17
  (1 shorter events, 0.0 us)
Async XLA Ops:
  0.6 116.1 %copy-start = (bf16[64,128,128]{2,1,0:T(8,128)(2,1)S(1)}, bf16[64,128,128]{2,1,0:T(8,128)(2,1)}, u32[]{:S(2)}) copy-start(bf16[64,128,128]{2,1,0:T(8,128)(2,1)} %h_hbm.1) | copy-start | bytes 6291460
  0.6 116.1 %copy-start.1 = (s32[8,4]{0,1:T(4,128)S(1)}, s32[8,4]{0,1:T(4,128)}, u32[]{:S(2)}) copy-start(s32[8,4]{0,1:T(4,128)} %param.14) | copy-start | bytes 388
  0.7 116.1 %copy-start.2 = (s32[8,4]{0,1:T(4,128)S(1)}, s32[8,4]{0,1:T(4,128)}, u32[]{:S(2)}) copy-start(s32[8,4]{0,1:T(4,128)} %param.15) | copy-start | bytes 388
  0.7 116.1 %copy-start.3 = (s32[8,4]{0,1:T(4,128)S(1)}, s32[8,4]{0,1:T(4,128)}, u32[]{:S(2)}) copy-start(s32[8,4]{0,1:T(4,128)} %param.16) | copy-start | bytes 388
  0.7 116.1 %copy-start.4 = (bf16[1024]{0:T(1024)(128)(2,1)S(1)}, bf16[1024]{0:T(1024)(128)(2,1)}, u32[]{:S(2)}) copy-start(bf16[1024]{0:T(1024)(128)(2,1)} %param.17) | copy-start | bytes 6148
  0.7 116.1 %copy-start.5 = (s32[1,32,1]{1,2,0:T(1,128)S(1)}, s32[1,32,1]{1,2,0:T(1,128)}, u32[]{:S(2)}) copy-start(s32[1,32,1]{1,2,0:T(1,128)} %param.18) | copy-start | bytes 388
  0.7 116.1 %copy-start.6 = (s32[1,32]{1,0:T(1,128)S(1)}, s32[1,32]{1,0:T(1,128)}, u32[]{:S(2)}) copy-start(s32[1,32]{1,0:T(1,128)} %wanted.1) | copy-start | bytes 388

commit v5 on v4

--- a/solution.py
+++ b/solution.py
@@ -430,38 +430,67 @@
     for i in range(1, ROWS):
         row_copy(i).start()
 
-    dens[QB * 8] = jnp.zeros((BS, BS), jnp.bfloat16)
-    get_h.wait()
-    get_s.wait()
-    pltpu.make_async_copy(e_in, e_in, e_sem).wait()
-    get_table = pltpu.make_async_copy(e_in, e_table, local_sem.at[5])
-    get_table.start()
-    get_table.wait()
-    for i in range(1, ROWS):
-        row_arrival(i).wait()
-
-    eye = lax.broadcasted_iota(jnp.int32, (BS, BS), 0) == lax.broadcasted_iota(
-        jnp.int32, (BS, BS), 1
-    )
-
-    def weigh(src, carry):
-        for k in range(CAP):
-            line = e_rows[src // COLS, pl.ds(e_table[src, 0, k] // QB, 1), :]
-            line = jnp.broadcast_to(line, (BS, BS))
-            col = jnp.sum(jnp.where(eye, line, 0.0), axis=1, keepdims=True)
-            s = src * CAP + k
-            wbuf[s] = hbuf[s].astype(jnp.float32) - col * sbuf[s].astype(jnp.float32)
-        return carry
-
-    lax.fori_loop(0, DEVICES, weigh, 0)
-
-    wrong = jnp.int32(0)
-    for src in range(DEVICES):
-        mine, other = e_table[src, 0, CAP], e_table[src + 1 - 2 * (src % 2), 0, CAP]
-        over = (mine > room).astype(jnp.int32) * (mine - room)
-        free = (other < room).astype(jnp.int32) * (room - at_least(other, KEPT))
-        wrong = wrong + (over > free).astype(jnp.int32)
-    short[0] = (wrong > 0).astype(jnp.int32)
+    def pass_on(d, ch):
+        @pl.when(z >= d)
+        def _():
+            up(d - 1, ch).wait_recv()
+            if d < LINE - 1:
+
+                @pl.when(z < LINE - 1)
+                def _():
+                    up(d, ch).start()
+
+            twin(d, ch).start()
+
+        @pl.when(z + d < LINE)
+        def _():
+            down(d - 1, ch).wait_recv()
+            if d < LINE - 1:
+
+                @pl.when(z > 0)
+                def _():
+                    down(d, ch).start()
+
+            twin(LINE - 1 + d, ch).start()
+
+    def wait_twin(i):
+        loop(0, PIECES, lambda ch: from_twin(i, ch).wait())
+
+    def expand(ref, panel, ch):
+        for i in range(STEP // BS):
+            row = ch * (STEP // BS) + i
+            for j in range(QB):
+                block = ref[place[panel, j * TALL + row]]
+                xg[panel, pl.ds(row * BS, BS), j * BS : (j + 1) * BS] = block
+
+    def multiply(zp, ch):
+        rows = pl.ds(ch * STEP, STEP)
+        return jnp.dot(
+            xg[2 * zp, rows, :], yg[zp, 0:HALF, :], preferred_element_type=jnp.float32
+        ) + jnp.dot(
+            xg[2 * zp + 1, rows, :], yg[zp, HALF : 2 * HALF, :], preferred_element_type=jnp.float32
+        )
+
+    def add(d):
+        def panels(zp, i):
+            wait_twin(i)
+
+            def one(ch):
+                expand(lines[i], 2 * zp, ch)
+                expand(lines[i], 2 * zp + 1, ch)
+                acc[pl.ds(ch * STEP, STEP), :] += multiply(zp, ch)
+
+            loop(0, CHUNKS, one)
+
+        @pl.when(z >= d)
+        def _():
+            panels(z - d, d)
+
+        @pl.when(z + d < LINE)
+        def _():
+            panels(z + d, LINE - 1 + d)
+
+    loop(0, 1, lambda ch: pass_on(1, ch))
 
     pltpu.make_async_copy(t_in, t_in, t_sem).wait()
     get_pats = pltpu.make_async_copy(t_in, pats, local_sem.at[5])
@@ -497,73 +526,46 @@
 
     loop(0, COLS, locate)
 
-    def pass_on(d, ch):
-        @pl.when(z >= d)
-        def _():
-            up(d - 1, ch).wait_recv()
-            if d < LINE - 1:
-
-                @pl.when(z < LINE - 1)
-                def _():
-                    up(d, ch).start()
-
-            twin(d, ch).start()
-
-        @pl.when(z + d < LINE)
-        def _():
-            down(d - 1, ch).wait_recv()
-            if d < LINE - 1:
-
-                @pl.when(z > 0)
-                def _():
-                    down(d, ch).start()
-
-            twin(LINE - 1 + d, ch).start()
-
-    def wait_twin(i):
-        loop(0, PIECES, lambda ch: from_twin(i, ch).wait())
-
-    def expand(ref, panel, ch):
-        for i in range(STEP // BS):
-            row = ch * (STEP // BS) + i
-            for j in range(QB):
-                block = ref[place[panel, j * TALL + row]]
-                xg[panel, pl.ds(row * BS, BS), j * BS : (j + 1) * BS] = block
-
-    def multiply(zp, ch):
-        rows = pl.ds(ch * STEP, STEP)
-        return jnp.dot(
-            xg[2 * zp, rows, :], yg[zp, 0:HALF, :], preferred_element_type=jnp.float32
-        ) + jnp.dot(
-            xg[2 * zp + 1, rows, :], yg[zp, HALF : 2 * HALF, :], preferred_element_type=jnp.float32
-        )
-
-    def add(d):
-        def panels(zp, i):
-            wait_twin(i)
-
-            def one(ch):
-                expand(lines[i], 2 * zp, ch)
-                expand(lines[i], 2 * zp + 1, ch)
-                acc[pl.ds(ch * STEP, STEP), :] += multiply(zp, ch)
-
-            loop(0, CHUNKS, one)
-
-        @pl.when(z >= d)
-        def _():
-            panels(z - d, d)
-
-        @pl.when(z + d < LINE)
-        def _():
-            panels(z + d, LINE - 1 + d)
-
-    loop(0, 1, lambda ch: pass_on(1, ch))
+    loop(1, PIECES, lambda ch: pass_on(1, ch))
+
+    dens[QB * 8] = jnp.zeros((BS, BS), jnp.bfloat16)
+    get_h.wait()
+    get_s.wait()
+    pltpu.make_async_copy(e_in, e_in, e_sem).wait()
+    get_table = pltpu.make_async_copy(e_in, e_table, local_sem.at[5])
+    get_table.start()
+    get_table.wait()
+    for i in range(1, ROWS):
+        row_arrival(i).wait()
+
+    eye = lax.broadcasted_iota(jnp.int32, (BS, BS), 0) == lax.broadcasted_iota(
+        jnp.int32, (BS, BS), 1
+    )
+
+    def weigh(src, carry):
+        for k in range(CAP):
+            line = e_rows[src // COLS, pl.ds(e_table[src, 0, k] // QB, 1), :]
+            line = jnp.broadcast_to(line, (BS, BS))
+            col = jnp.sum(jnp.where(eye, line, 0.0), axis=1, keepdims=True)
+            s = src * CAP + k
+            wbuf[s] = hbuf[s].astype(jnp.float32) - col * sbuf[s].astype(jnp.float32)
+        return carry
+
+    lax.fori_loop(0, DEVICES, weigh, 0)
+
+    wrong = jnp.int32(0)
+    for src in range(DEVICES):
+        mine, other = e_table[src, 0, CAP], e_table[src + 1 - 2 * (src % 2), 0, CAP]
+        over = (mine > room).astype(jnp.int32) * (mine - room)
+        free = (other < room).astype(jnp.int32) * (room - at_least(other, KEPT))
+        wrong = wrong + (over > free).astype(jnp.int32)
+    short[0] = (wrong > 0).astype(jnp.int32)
+
     y_copy(row_x, 0, r, 0).wait_recv()
     y_copy(row_x, 0, row_y, 4).start()
     y_copy(row_y, 1, r, 1).wait_recv()
     y_copy(row_y, 1, row_x, 5).start()
-    loop(1, PIECES, lambda ch: pass_on(1, ch))
-    loop(0, 1, lambda ch: pass_on(2, ch))
+    loop(0, PIECES, lambda ch: pass_on(2, ch))
     y_copy(row_x, 1, r, 2).wait_recv()
     y_copy(row_y, 0, r, 3).wait_recv()
     row_d = 3 - r
@@ -577,7 +579,6 @@
 
     loop(0, CHUNKS, first)
     add(1)
-    loop(1, PIECES, lambda ch: pass_on(2, ch))
     add(2)
 
     eye_f = eye.astype(jnp.float32)

time: 119 us -> 113 us (0.950)
  Pallas kernels: 115 us -> 110 us
    pallas_call x1, Pallas kernels: 115 us -> 110 us  [fused(): pl.pallas_call(functools.partial(kernel, room), out_shape=(jax.ShapeDtype...]
where the time goes in v5:
time: 113 us
  Pallas kernels  110 us (97%)
  between operations  1.39 us (1%)
    pallas_call x1, Pallas kernels, fused(): pl.pallas_call(functools.partial(kernel, room), out_shape=(jax.ShapeDtype...  110 us

profile of v5, /device:TPU:1, one launch (start us, length us, event | category | flops | bytes accessed | tf_op | source)
XLA Modules:
  0.0 112.6 jit_solution(7368087962895342731)
XLA Ops:
  0.6 0.0 copy-start
  0.6 0.0 copy-start.1
  0.7 0.0 copy-start.2
  0.7 0.0 copy-start.3
  0.7 0.0 copy-start.4
  0.7 0.0 copy-start.5
  0.7 0.0 copy-start.6
  0.7 109.6 %room_22.1 = (bf16[1024,512]{1,0:T(8,128)(2,1)S(1)}, f32[64,128]{1,0:T(8,128)S(1)}, s32[1]{0:T(128)}) custom-call(s32[4,8]{1,0:T(4,128)} %bitcast.15, s32[4,8]{1,0:T(4,128)} %bitcast.19, s32[4,8]{1,0:T(4,128)} %bitcast.21, s32[1,32]{1,0:T(1,128)} %bitcast.25, s32[1,32]{1,0:T(1,128)} %wanted.1, s32[4,8]{1,0:T(4,128)} %bitcast.16, bf16[8,128]{1,0:T(8,128)(2,1)} %bitcast.23, ...), custom_call_target="tpu_custom_call" | custom-call | flops 4294967296 | bytes 8388608 | tf_op jit(solution)/shard_map/room_22/pallas_call | solution.py:723
  110.9 0.0 copy-done
  111.0 0.0 copy-done.1
  111.0 0.0 copy-done.2
  111.0 0.0 copy-done.3
  111.0 0.0 copy-done.4
  111.0 0.0 copy-done.5
  111.0 0.0 copy-done.6
  111.0 0.6 reduce_sum.16
  111.7 1.0 copy.17
  (1 shorter events, 0.0 us)
Async XLA Ops:
  0.6 110.3 %copy-start = (bf16[64,128,128]{2,1,0:T(8,128)(2,1)S(1)}, bf16[64,128,128]{2,1,0:T(8,128)(2,1)}, u32[]{:S(2)}) copy-start(bf16[64,128,128]{2,1,0:T(8,128)(2,1)} %h_hbm.1) | copy-start | bytes 6291460
  0.6 110.3 %copy-start.1 = (s32[8,4]{0,1:T(4,128)S(1)}, s32[8,4]{0,1:T(4,128)}, u32[]{:S(2)}) copy-start(s32[8,4]{0,1:T(4,128)} %param.14) | copy-start | bytes 388
  0.7 110.3 %copy-start.2 = (s32[8,4]{0,1:T(4,128)S(1)}, s32[8,4]{0,1:T(4,128)}, u32[]{:S(2)}) copy-start(s32[8,4]{0,1:T(4,128)} %param.15) | copy-start | bytes 388
  0.7 110.3 %copy-start.3 = (s32[8,4]{0,1:T(4,128)S(1)}, s32[8,4]{0,1:T(4,128)}, u32[]{:S(2)}) copy-start(s32[8,4]{0,1:T(4,128)} %param.16) | copy-start | bytes 388
  0.7 110.3 %copy-start.4 = (bf16[1024]{0:T(1024)(128)(2,1)S(1)}, bf16[1024]{0:T(1024)(128)(2,1)}, u32[]{:S(2)}) copy-start(bf16[1024]{0:T(1024)(128)(2,1)} %param.17) | copy-start | bytes 6148
  0.7 110.3 %copy-start.5 = (s32[1,32,1]{1,2,0:T(1,128)S(1)}, s32[1,32,1]{1,2,0:T(1,128)}, u32[]{:S(2)}) copy-start(s32[1,32,1]{1,2,0:T(1,128)} %param.18) | copy-start | bytes 388
  0.7 110.3 %copy-start.6 = (s32[1,32]{1,0:T(1,128)S(1)}, s32[1,32]{1,0:T(1,128)}, u32[]{:S(2)}) copy-start(s32[1,32]{1,0:T(1,128)} %wanted.1) | copy-start | bytes 388

commit v6 on v5

--- a/solution.py
+++ b/solution.py
@@ -336,17 +336,6 @@
         )
         hand_over.start()
     send_x(0)
-    if spill:
-        hand_over.wait_recv()
-        used = at_least(count, KEPT)
-
-        def fill(t):
-            own = (t < count).astype(jnp.int32)
-            extra = spill_in[own * spill + (1 - own) * (t - used) * (t >= used).astype(jnp.int32)]
-            lines[0][core * half + t] = xraw[listed[t]] + extra
-
-        loop(early, room, fill)
-    loop(1, PIECES, send_x)
     get_y.wait()
 
     def mask_y(i):
@@ -362,6 +351,17 @@
     y_copy(r, 1, row_x, 2).start()
     y_copy(r, 0, row_y, 3).start()
 
+    if spill:
+        hand_over.wait_recv()
+        used = at_least(count, KEPT)
+
+        def fill(t):
+            own = (t < count).astype(jnp.int32)
+            extra = spill_in[own * spill + (1 - own) * (t - used) * (t >= used).astype(jnp.int32)]
+            lines[0][core * half + t] = xraw[listed[t]] + extra
+
+        loop(early, room, fill)
+    loop(1, PIECES, send_x)
     def mask_x(i):
         rows = pl.ds(i * BS, BS)
         for j in range(QB):

time: 113 us -> 111 us (0.982)
  Pallas kernels: 110 us -> 108 us
    pallas_call x1, Pallas kernels: 110 us -> 108 us  [fused(): pl.pallas_call(functools.partial(kernel, room), out_shape=(jax.ShapeDtype...]
where the time goes in v6:
time: 111 us
  Pallas kernels  108 us (97%)
  between operations  1.39 us (1%)
    pallas_call x1, Pallas kernels, fused(): pl.pallas_call(functools.partial(kernel, room), out_shape=(jax.ShapeDtype...  108 us

profile of v6, /device:TPU:1, one launch (start us, length us, event | category | flops | bytes accessed | tf_op | source)
XLA Modules:
  0.0 111.0 jit_solution(8050191193520880961)
XLA Ops:
  0.6 0.0 copy-start
  0.6 0.0 copy-start.1
  0.7 0.0 copy-start.2
  0.7 0.0 copy-start.3
  0.7 0.0 copy-start.4
  0.7 0.0 copy-start.5
  0.7 0.0 copy-start.6
  0.7 108.0 %room_22.1 = (bf16[1024,512]{1,0:T(8,128)(2,1)S(1)}, f32[64,128]{1,0:T(8,128)S(1)}, s32[1]{0:T(128)}) custom-call(s32[4,8]{1,0:T(4,128)} %bitcast.15, s32[4,8]{1,0:T(4,128)} %bitcast.19, s32[4,8]{1,0:T(4,128)} %bitcast.21, s32[1,32]{1,0:T(1,128)} %bitcast.25, s32[1,32]{1,0:T(1,128)} %wanted.1, s32[4,8]{1,0:T(4,128)} %bitcast.16, bf16[8,128]{1,0:T(8,128)(2,1)} %bitcast.23, ...), custom_call_target="tpu_custom_call" | custom-call | flops 4294967296 | bytes 8388608 | tf_op jit(solution)/shard_map/room_22/pallas_call | solution.py:723
  109.4 0.0 copy-done
  109.4 0.0 copy-done.1
  109.4 0.0 copy-done.2
  109.4 0.0 copy-done.3
  109.4 0.0 copy-done.4
  109.4 0.0 copy-done.5
  109.4 0.0 copy-done.6
  109.5 0.6 reduce_sum.16
  110.1 1.0 copy.17
  (1 shorter events, 0.0 us)
Async XLA Ops:
  0.6 108.7 %copy-start = (bf16[64,128,128]{2,1,0:T(8,128)(2,1)S(1)}, bf16[64,128,128]{2,1,0:T(8,128)(2,1)}, u32[]{:S(2)}) copy-start(bf16[64,128,128]{2,1,0:T(8,128)(2,1)} %h_hbm.1) | copy-start | bytes 6291460
  0.6 108.7 %copy-start.1 = (s32[8,4]{0,1:T(4,128)S(1)}, s32[8,4]{0,1:T(4,128)}, u32[]{:S(2)}) copy-start(s32[8,4]{0,1:T(4,128)} %param.14) | copy-start | bytes 388
  0.7 108.7 %copy-start.2 = (s32[8,4]{0,1:T(4,128)S(1)}, s32[8,4]{0,1:T(4,128)}, u32[]{:S(2)}) copy-start(s32[8,4]{0,1:T(4,128)} %param.15) | copy-start | bytes 388
  0.7 108.7 %copy-start.3 = (s32[8,4]{0,1:T(4,128)S(1)}, s32[8,4]{0,1:T(4,128)}, u32[]{:S(2)}) copy-start(s32[8,4]{0,1:T(4,128)} %param.16) | copy-start | bytes 388
  0.7 108.7 %copy-start.4 = (bf16[1024]{0:T(1024)(128)(2,1)S(1)}, bf16[1024]{0:T(1024)(128)(2,1)}, u32[]{:S(2)}) copy-start(bf16[1024]{0:T(1024)(128)(2,1)} %param.17) | copy-start | bytes 6148
  0.7 108.7 %copy-start.5 = (s32[1,32,1]{1,2,0:T(1,128)S(1)}, s32[1,32,1]{1,2,0:T(1,128)}, u32[]{:S(2)}) copy-start(s32[1,32,1]{1,2,0:T(1,128)} %param.18) | copy-start | bytes 388
  0.7 108.7 %copy-start.6 = (s32[1,32]{1,0:T(1,128)S(1)}, s32[1,32]{1,0:T(1,128)}, u32[]{:S(2)}) copy-start(s32[1,32]{1,0:T(1,128)} %wanted.1) | copy-start | bytes 388
